TPU v7x, 256 devices: a whole 4x4x8 slice. The times are simulated.
256 devices in a mesh: replica: 16 (over z, core), fsdp: 4 (over y), tensor: 4 (over x).
Axes of the slice: x: 4, y: 4, z: 8, core: 2. Of those that a mesh axis runs over, the one named last changes fastest.
Arguments:
- activations: bfloat16 [32768, 8192], P(('replica', 'fsdp', 'tensor')), may hold values from -6 to 6
- cotangent: bfloat16 [32768, 2048], P(('replica', 'fsdp'), 'tensor'), may hold values from -0.625 to 0.625
- momentum: float32 [16, 8192, 2048], P('replica', 'fsdp', 'tensor'), may hold values from -6 to 6
- band_index: int32 [16, 128, 32, 16], P('replica', 'fsdp', 'tensor'), may hold values from 0 to 975, as said below
Outputs:
- new_momentum: float32 [16, 8192, 2048], P('replica', 'fsdp', 'tensor')
- update: bfloat16 [8192, 2048], P('fsdp', 'tensor')
Inputs may be any that keep to these rules, and one draw needn't show every extreme that they name: `band_index`: within each block the 16 indices of a replica are distinct, and each is k1 * 64 + k2 with k1 and k2 below 16.
All inputs are finite; a program needn't handle non-finite values.
Results may differ from a plain program's by a relative error of at most 0.0011.
Values may be sent and summed in bfloat16 or wider, within the bound.
No kernel may reach another device: no remote copies, remote signals or barrier semaphores. Data moves between devices by JAX's collectives and lax.ppermute only.
A program may use at most 128 MiB of HBM per device.

v0:
```python
import functools

import jax
import jax.numpy as jnp
import ml_dtypes
import numpy as np
from jax import lax
from jax.experimental import pallas as pl
from jax.experimental.pallas import tpu as pltpu
from jax.sharding import PartitionSpec as P

SPAN = 64
LOW = 16
TILE = 256
DECAY = 0.999
VMEM_LIMIT = 40 * 1024 * 1024
VMEM = pl.BlockSpec(memory_space=pltpu.VMEM)
HBM = pl.BlockSpec(memory_space=pltpu.HBM)
SMEM = pl.BlockSpec(memory_space=pltpu.SMEM)
PARAMS = pltpu.CompilerParams(vmem_limit_bytes=VMEM_LIMIT)


def split_table(table):
    high = table.astype(ml_dtypes.bfloat16)
    low = (table - high.astype(np.float64)).astype(ml_dtypes.bfloat16)
    return high, low


def tables(cols):
    frequency = np.arange(LOW)[:, None]
    position = np.arange(SPAN)[None, :]
    cosine = np.cos(np.pi * (2.0 * position + 1.0) * frequency / (2.0 * SPAN))
    cosine = cosine * np.where(frequency == 0, np.sqrt(1.0 / SPAN), np.sqrt(2.0 / SPAN))
    down_high, down_low = split_table(np.kron(np.eye(TILE // SPAN), cosine))
    across_high, across_low = split_table(np.kron(np.eye(cols // SPAN), cosine))
    table = np.zeros((640, cols), ml_dtypes.bfloat16)
    table[:128] = across_high
    table[128:256] = across_low
    table[256:320, :TILE], table[320:384, :TILE] = down_high, down_low
    table[384:, :192] = np.concatenate([down_high.T, down_high.T, down_low.T], 1)
    return table


def halves(x):
    high = x.astype(jnp.bfloat16)
    return high, (x - high.astype(jnp.float32)).astype(jnp.bfloat16)


def dot(a, b):
    return jnp.dot(a, b, preferred_element_type=jnp.float32)


def forward(x, table):
    x_high, x_low = halves(x)
    both = dot(table[256:384, :TILE], x_high)
    down_high, down_low = halves(both[:64] + both[64:] + dot(table[256:320, :TILE], x_low))
    turned = (((1,), (1,)), ((), ()))
    stack = jnp.concatenate([down_high, down_low], 0)
    both = lax.dot_general(stack, table[:128, :], turned, preferred_element_type=jnp.float32)
    low = lax.dot_general(down_high, table[128:256, :], turned, preferred_element_type=jnp.float32)
    return both[:64] + both[64:] + low


def backward(coefficients, table):
    high, low = halves(coefficients)
    both = dot(jnp.concatenate([high, low], 0), table[:128, :])
    high, low = halves(both[:64] + both[64:] + dot(high, table[128:256, :]))
    return dot(table[384:, :192], jnp.concatenate([high, low, high], 0))


def order_kernel(place_ref, *refs):
    parts, out_ref = refs[:4], refs[4]
    tensor, sign = place_ref[0], place_ref[1]
    for shift in range(4):
        start = lax.rem(tensor + 4 - sign * shift, 4) * 128
        for d in range(4):
            out_ref[pl.ds((shift * 4 + d) * 128, 128), :] = parts[d][pl.ds(pl.multiple_of(start, 128), 128), :]


def mask_kernel(index_ref, pick_ref, out_ref):
    index = index_ref[...]
    place = index // SPAN * LOW + index % SPAN
    wide = lax.dot_general(
        place.astype(jnp.bfloat16),
        pick_ref[...],
        (((0,), (0,)), ((), ())),
        preferred_element_type=jnp.float32,
    )
    span_rows = index.shape[1]
    lanes = out_ref.shape[1]
    k1 = lax.broadcasted_iota(jnp.int32, (span_rows, LOW, lanes), 1)
    k2 = lax.rem(lax.broadcasted_iota(jnp.int32, (span_rows, LOW, lanes), 2), LOW)
    here = (k1 * LOW + k2).astype(jnp.float32)
    mask = jnp.zeros(here.shape, jnp.float32)
    for j in range(pick_ref.shape[1] // lanes):
        row = wide[:, j * lanes : (j + 1) * lanes]
        mask = jnp.where(row[:, None, :] == here, 1.0, mask)
    out_ref[...] = mask.reshape(out_ref.shape)


def chunk_kernel(*refs):
    own, others = refs[:4], refs[4:8]
    cot_ref, momentum_ref, mask_ref, table = refs[8:12]
    new_ref, kept_ref, lhs = refs[-3:]
    for shift in range(4):
        lhs[pl.ds(shift * 512, 128), :] = own[shift][...]
        lhs[pl.ds(shift * 512 + 128, 384), :] = others[shift][...]
    gradient = lax.dot_general(
        lhs[...], cot_ref[...], (((0,), (0,)), ((), ())), preferred_element_type=jnp.float32
    )
    blended = DECAY * momentum_ref[...] + gradient
    kept = forward(blended, table) * mask_ref[...]
    kept_ref[...] = kept
    new_ref[...] = blended - backward(kept, table)


def chunk(first, steps, own, others, cot, momentum, mask, table, previous, *before):
    rows, cols = momentum.shape
    low_rows, low_cols = TILE // SPAN * LOW, cols // SPAN * LOW
    in_specs = [pl.BlockSpec((128, TILE), lambda i: (0, first + i))] * 4
    in_specs += [pl.BlockSpec((384, TILE), lambda i: (0, i))] * 4
    in_specs += [
        pl.BlockSpec(cot.shape, lambda i: (0, 0)),
        pl.BlockSpec((TILE, cols), lambda i: (first + i, 0)),
        pl.BlockSpec((low_rows, low_cols), lambda i: (first + i, 0)),
        pl.BlockSpec(table.shape, lambda i: (0, 0)),
    ]
    args = [*own, *others, cot, momentum, mask, table, *before]
    aliases = {}
    if previous is not None:
        aliases = {len(args): 0}
        args.append(previous)
    return pl.pallas_call(
        chunk_kernel,
        grid=(steps,),
        in_specs=in_specs + [HBM] * (len(args) - 12),
        out_specs=[
            pl.BlockSpec((TILE, cols), lambda i: (first + i, 0)),
            pl.BlockSpec((low_rows, low_cols), lambda i: (i, 0)),
        ],
        out_shape=[
            jax.ShapeDtypeStruct((rows, cols), jnp.float32),
            jax.ShapeDtypeStruct((steps * low_rows, low_cols), jnp.float32),
        ],
        scratch_shapes=[pltpu.VMEM((2048, TILE), jnp.bfloat16)],
        input_output_aliases=aliases,
        compiler_params=PARAMS,
        cost_estimate=pl.CostEstimate(
            flops=2 * 2048 * TILE * cols * 2 * steps, bytes_accessed=steps * 3 * 2**20, transcendentals=0
        ),
        name=f"chunk{first}",
    )(*args)


def spread_kernel(first, steps, coefficients_ref, table, *refs):
    out_ref, made, sems = refs[-3:]
    low_rows = TILE // SPAN * LOW
    copies = []
    for i in range(steps):
        part = coefficients_ref[pl.ds(i * low_rows, low_rows), :]
        made[i] = backward(part, table).astype(made.dtype)
        rows = pl.ds((first + i) * TILE, TILE)
        copies.append(pltpu.make_async_copy(made.at[i], out_ref.at[rows, :], sems.at[i]))
        copies[-1].start()
    for copy in copies:
        copy.wait()


def spread(coefficients, shape, table):
    rows, cols = shape
    steps = rows // TILE
    return pl.pallas_call(
        lambda *refs: spread_kernel(0, steps, *refs),
        in_specs=[VMEM] * 2,
        out_specs=HBM,
        out_shape=jax.ShapeDtypeStruct(shape, jnp.bfloat16),
        scratch_shapes=[pltpu.VMEM((steps, TILE, cols), jnp.bfloat16), pltpu.SemaphoreType.DMA((steps,))],
        compiler_params=PARAMS,
        cost_estimate=pl.CostEstimate(flops=steps * 10**8, bytes_accessed=steps * 2**18, transcendentals=0),
        name="spread",
    )(coefficients, table)


def pack_kernel(*refs, start, places):
    out, held, loads, stores = refs[-4:]
    rows, width = refs[0].shape[0], out.shape[1]
    coming, going = [], []
    for i in range(places):
        here = held.at[pl.ds(i * rows, rows), :]
        coming.append(pltpu.make_async_copy(refs[i].at[:, pl.ds(start, width)], here, loads.at[i]))
        going.append(pltpu.make_async_copy(here, out.at[pl.ds(i * rows, rows), :], stores.at[i]))
        coming[-1].start()
    for i in range(places):
        coming[i].wait()
        going[i].start()
    for i in range(places):
        going[i].wait()


def pack(parts, start, width, *before):
    places, rows = len(parts), parts[0].shape[0]
    return pl.pallas_call(
        functools.partial(pack_kernel, start=start, places=places),
        in_specs=[HBM] * (places + len(before)),
        out_specs=HBM,
        out_shape=jax.ShapeDtypeStruct((places * rows, width), parts[0].dtype),
        scratch_shapes=[
            pltpu.VMEM((places * rows, width), parts[0].dtype),
            pltpu.SemaphoreType.DMA((places,)),
            pltpu.SemaphoreType.DMA((places,)),
        ],
        compiler_params=PARAMS,
        name="pack",
    )(*parts, *before)


def after(x, *before):
    return pl.pallas_call(
        lambda *refs: None,
        in_specs=[HBM] * (1 + len(before)),
        out_specs=HBM,
        out_shape=jax.ShapeDtypeStruct(x.shape, x.dtype),
        input_output_aliases={0: 0},
        compiler_params=PARAMS,
        name="after",
    )(x, *before)


def apart(x, axis, by):
    pairs = []
    for replica in range(16):
        step = by if replica % 2 == 0 else -by
        pairs += [(replica * 4 + i, replica * 4 + (i + step) % 4) for i in range(4)]
    return lax.ppermute(x, ("replica", axis), pairs)


def around(x, axis, mirrored=False):
    one = apart(x, axis, 1)
    three = apart(x, axis, -1)
    two = apart(three, axis, -1) if mirrored else apart(one, axis, 1)
    return [x, one, two, three]


def swapped(x, partner):
    pairs = []
    for i in range(16):
        z, core = partner(i // 2, i % 2)
        pairs.append((i, z * 2 + core))
    return lax.ppermute(x, "replica", pairs)


def over_replicas(x, core):
    half = x.shape[0] // 2
    mine = lax.dynamic_slice(x, (core * half, 0), (half, x.shape[1]))
    theirs = lax.dynamic_slice(x, ((1 - core) * half, 0), (half, x.shape[1]))
    mine = mine + swapped(theirs, lambda z, c: (z, 1 - c))
    def quad(z, c):
        return (((z - 2 * c) % 8 ^ 2) + 2 * c) % 8, c

    for partner in (lambda z, c: (z ^ 1, c), quad, lambda z, c: ((7 + 4 * c - z) % 8, c)):
        mine = mine + swapped(mine, partner)
    other = swapped(mine, lambda z, c: (z, 1 - c))
    return jnp.where(core == 0, jnp.concatenate([mine, other], 0), jnp.concatenate([other, mine], 0))


def pick_table(span_cols, band):
    pick = np.zeros((span_cols, band, band, span_cols, LOW), np.float32)
    for b in range(span_cols):
        for j in range(band):
            pick[b, j, j, b, :] = 1.0
    return pick.reshape(span_cols * band, band * span_cols * LOW).astype(ml_dtypes.bfloat16)


def local(activations, cotangent, momentum, band_index):
    momentum, band_index = momentum[0], band_index[0]
    rows, cols = momentum.shape
    span_rows, span_cols, band = band_index.shape
    fsdp = lax.axis_index("fsdp")
    tensor = lax.axis_index("tensor")
    core = lax.rem(lax.axis_index("replica"), 2)
    sign = 1 - 2 * core
    table = jnp.asarray(tables(cols))

    def columns(d, start, width):
        owner = lax.rem(fsdp + 4 + sign * d, 4)
        return lax.dynamic_slice(activations, (0, owner * rows + start), (activations.shape[0], width))

    mine = columns(0, 0, rows)
    own = around(mine, "tensor")
    pieces = [columns(d, 0, 768) for d in (1, 2, 3)] + [columns(d, 768, 1280) for d in (1, 2, 3)]
    early = [apart(pieces[d - 1], "fsdp", d) for d in (1, 2, 3)]
    late_one = apart(after(pieces[3], own[1], *early), "fsdp", 1)
    late_three = apart(after(pieces[5], own[1], *early), "fsdp", 3)
    late = [late_one, apart(after(pieces[4], late_one), "fsdp", 2), late_three]
    cots = around(pack([cotangent], 0, cols, late_one), "fsdp")

    chunks = [(0, 3), (3, 2), (5, 3)]
    units = [own]
    for first, steps in chunks:
        if first == 0:
            unit = pack(early, 0, 768, own[1], own[3])
        else:
            before = [units[-1][1], units[-1][3]] if first == 3 else [own[2], units[-2][2], units[-1][1]]
            unit = pack(late, first * TILE - 768, steps * TILE, *before)
        units.append(around(unit, "tensor", first in (0, 5)))
    others = units[1:]

    cot = pl.pallas_call(
        order_kernel,
        in_specs=[SMEM] + [VMEM] * 4,
        out_specs=VMEM,
        out_shape=jax.ShapeDtypeStruct((2048, cols), jnp.bfloat16),
        compiler_params=PARAMS,
        name="order",
    )(jnp.stack([tensor, sign]).astype(jnp.int32), *cots)

    mask = pl.pallas_call(
        mask_kernel,
        in_specs=[VMEM] * 2,
        out_specs=VMEM,
        out_shape=jax.ShapeDtypeStruct((span_rows * LOW, span_cols * LOW), jnp.float32),
        compiler_params=PARAMS,
        name="mask",
    )(band_index.transpose(1, 2, 0).reshape(span_cols * band, span_rows), jnp.asarray(pick_table(span_cols, band)))

    def part(i, previous, *before):
        first, steps = chunks[i]
        return chunk(first, steps, own, others[i], cot, momentum, mask, table, previous, *before)

    new_momentum, kept = None, []
    for i in range(len(chunks)):
        new_momentum, kept_i = part(i, new_momentum)
        kept.append(kept_i)
    combined = over_replicas(jnp.concatenate(kept, 0), core)
    update = spread(combined, (rows, cols), table)
    return (new_momentum[None], update)


def solution(mesh):
    in_specs = (
        P(("replica", "fsdp", "tensor"), None),
        P(("replica", "fsdp"), "tensor"),
        P("replica", "fsdp", "tensor"),
        P("replica", "fsdp", "tensor", None),
    )
    out_specs = (P("replica", "fsdp", "tensor"), P("fsdp", "tensor"))
    return jax.shard_map(local, mesh=mesh, in_specs=in_specs, out_specs=out_specs, check_vma=False)
```

profile of v0, /device:TPU:57, one launch (start us, length us, event | category | flops | bytes accessed | tf_op | source)
XLA Modules:
  0.0 129.0 jit_solution(6332965561008045808)
XLA Ops:
  1.7 2.6 %collective-permute-start = (bf16[128,2048]{1,0:T(8,128)(2,1)S(1)}, bf16[128,2048]{1,0:T(8,128)(2,1)S(1)}, u32[]{:S(2)}, u32[]{:S(2)}) collective-permute-start(bf16[128,2048]{1,0:T(8,128)(2,1)S(1)} %constant_dynamic-slice_fusion.7.refs_0_), channel_id=1, source_target_pairs={{0,1},{1,2},{2,3},{3,0},{16,19},{17,16},{18,17},{19,18},{32,33},{3... | collective-permute-start | bytes 1572872 | tf_op jit(solution)/shard_map/ppermute | solution.py:234
  4.3 1.2 constant_dynamic-slice_fusion.3
  6.7 1.9 %collective-permute-start.5 = (bf16[128,768]{1,0:T(8,128)(2,1)S(1)}, bf16[128,768]{1,0:T(8,128)(2,1)S(1)}, u32[]{:S(2)}, u32[]{:S(2)}) collective-permute-start(bf16[128,768]{1,0:T(8,128)(2,1)S(1)} %get-tuple-element.17), channel_id=1, source_target_pairs={{0,12},{4,0},{8,4},{12,8},{16,20},{20,24},{24,28},{28,16},{32,44},... | collective-permute-start | bytes 589832 | tf_op jit(solution)/shard_map/ppermute | solution.py:234
  8.6 8.4 %collective-permute-done.3.refs_2_.refs_0_ = bf16[128,768]{1,0:T(8,128)(2,1)S(1)} collective-permute-done((bf16[128,768]{1,0:T(8,128)(2,1)S(1)}, bf16[128,768]{1,0:T(8,128)(2,1)S(1)}, u32[]{:S(2)}, u32[]{:S(2)}) %collective-permute-start.3) | collective-permute-done | bytes 196640 | tf_op jit(solution)/shard_map/ppermute | solution.py:234
  17.0 1.1 collective-permute-done.5.refs_4_.refs_2_
  18.1 1.6 %pack.4.refs_4_ = bf16[384,768]{1,0:T(8,128)(2,1)S(1)} custom-call(bf16[128,768]{1,0:T(8,128)(2,1)S(1)} %collective-permute-done.3.refs_2_.refs_0_, bf16[128,768]{1,0:T(8,128)(2,1)S(1)} %collective-permute-done.4.refs_3_.refs_1_, bf16[128,768]{1,0:T(8,128)(2,1)S(1)} %collective-permute-done.5.refs_4_.refs_2_, ...), custom_call_target="tpu_custom_call" | custom-call | tf_op jit(solution)/shard_map/pack/pallas_call | solution.py:202
  19.9 1.2 constant_dynamic-slice_fusion.1
  21.9 2.5 %collective-permute-start.11 = (bf16[384,768]{1,0:T(8,128)(2,1)S(1)}, bf16[384,768]{1,0:T(8,128)(2,1)S(1)}, u32[]{:S(2)}, u32[]{:S(2)}) collective-permute-start(bf16[384,768]{1,0:T(8,128)(2,1)S(1)} %pack.4.refs_4_), channel_id=1, source_target_pairs={{0,1},{1,2},{2,3},{3,0},{16,19},{17,16},{18,17},{19,18},{32,33},{3... | collective-permute-start | bytes 1769480 | tf_op jit(solution)/shard_map/ppermute | solution.py:234
  24.5 2.0 %collective-permute-start.8 = (bf16[128,1280]{1,0:T(8,128)(2,1)S(1)}, bf16[128,1280]{1,0:T(8,128)(2,1)S(1)}, u32[]{:S(2)}, u32[]{:S(2)}) collective-permute-start(bf16[128,1280]{1,0:T(8,128)(2,1)S(1)} %after.5), channel_id=1, source_target_pairs={{0,12},{4,0},{8,4},{12,8},{16,20},{20,24},{24,28},{28,16},{32,44},... | collective-permute-start | bytes 983048 | tf_op jit(solution)/shard_map/ppermute | solution.py:234
  26.4 2.0 %collective-permute-done.6.refs_1_.refs_0_ = bf16[128,1280]{1,0:T(8,128)(2,1)S(1)} collective-permute-done((bf16[128,1280]{1,0:T(8,128)(2,1)S(1)}, bf16[128,1280]{1,0:T(8,128)(2,1)S(1)}, u32[]{:S(2)}, u32[]{:S(2)}) %collective-permute-start.6) | collective-permute-done | bytes 327712 | tf_op jit(solution)/shard_map/ppermute | solution.py:234
  28.5 2.1 %collective-permute-done.9.refs_4_.refs_7_ = bf16[384,768]{1,0:T(8,128)(2,1)S(1)} collective-permute-done((bf16[384,768]{1,0:T(8,128)(2,1)S(1)}, bf16[384,768]{1,0:T(8,128)(2,1)S(1)}, u32[]{:S(2)}, u32[]{:S(2)}) %collective-permute-start.9) | collective-permute-done | bytes 589856 | tf_op jit(solution)/shard_map/ppermute | solution.py:234
  30.6 2.7 %collective-permute-start.1 = (bf16[128,2048]{1,0:T(8,128)(2,1)S(1)}, bf16[128,2048]{1,0:T(8,128)(2,1)S(1)}, u32[]{:S(2)}, u32[]{:S(2)}) collective-permute-start(bf16[128,2048]{1,0:T(8,128)(2,1)S(1)} %collective-permute-done.refs_1_.refs_3_), channel_id=1, source_target_pairs={{0,1},{1,2},{2,3},{3,0},{16,19},{17,16},{18,17},{19,18},{32,33},{3... | collective-permute-start | bytes 1572872 | tf_op jit(solution)/shard_map/ppermute | solution.py:234
  34.0 2.3 %collective-permute-done.11.refs_3_.refs_5_ = bf16[384,768]{1,0:T(8,128)(2,1)S(1)} collective-permute-done((bf16[384,768]{1,0:T(8,128)(2,1)S(1)}, bf16[384,768]{1,0:T(8,128)(2,1)S(1)}, u32[]{:S(2)}, u32[]{:S(2)}) %collective-permute-start.11) | collective-permute-done | bytes 589856 | tf_op jit(solution)/shard_map/ppermute | solution.py:234
  36.8 3.2 %collective-permute-start.12 = (bf16[384,512]{1,0:T(8,128)(2,1)S(1)}, bf16[384,512]{1,0:T(8,128)(2,1)S(1)}, u32[]{:S(2)}, u32[]{:S(2)}) collective-permute-start(bf16[384,512]{1,0:T(8,128)(2,1)S(1)} %pack.5.refs_4_), channel_id=1, source_target_pairs={{0,1},{1,2},{2,3},{3,0},{16,19},{17,16},{18,17},{19,18},{32,33},{3... | collective-permute-start | bytes 1179656 | tf_op jit(solution)/shard_map/ppermute | solution.py:234
  40.0 4.3 %collective-permute-done.1.refs_3_.refs_2_ = bf16[128,2048]{1,0:T(8,128)(2,1)S(1)} collective-permute-done((bf16[128,2048]{1,0:T(8,128)(2,1)S(1)}, bf16[128,2048]{1,0:T(8,128)(2,1)S(1)}, u32[]{:S(2)}, u32[]{:S(2)}) %collective-permute-start.1) | collective-permute-done | bytes 524320 | tf_op jit(solution)/shard_map/ppermute | solution.py:234
  44.4 8.1 %collective-permute-done.12.refs_5_ = bf16[384,512]{1,0:T(8,128)(2,1)S(1)} collective-permute-done((bf16[384,512]{1,0:T(8,128)(2,1)S(1)}, bf16[384,512]{1,0:T(8,128)(2,1)S(1)}, u32[]{:S(2)}, u32[]{:S(2)}) %collective-permute-start.12) | collective-permute-done | bytes 393248 | tf_op jit(solution)/shard_map/ppermute | solution.py:234
  53.6 2.7 %collective-permute-start.18 = (bf16[512,512]{1,0:T(8,128)(2,1)S(1)}, bf16[512,512]{1,0:T(8,128)(2,1)}, u32[]{:S(2)}, u32[]{:S(2)}) collective-permute-start(bf16[512,512]{1,0:T(8,128)(2,1)S(1)} %pack.7.refs_0_), channel_id=1, source_target_pairs={{0,12},{4,0},{8,4},{12,8},{16,20},{20,24},{24,28},{28,16},{32,44},... | collective-permute-start | bytes 1572872 | tf_op jit(solution)/shard_map/ppermute | solution.py:234
  59.2 2.7 %collective-permute-start.19 = (bf16[384,512]{1,0:T(8,128)(2,1)}, bf16[384,512]{1,0:T(8,128)(2,1)S(1)}, u32[]{:S(2)}, u32[]{:S(2)}) collective-permute-start(bf16[384,512]{1,0:T(8,128)(2,1)} %copy-done.4), channel_id=1, source_target_pairs={{0,1},{1,2},{2,3},{3,0},{16,19},{17,16},{18,17},{19,18},{32,33},{3... | collective-permute-start | bytes 1179656 | tf_op jit(solution)/shard_map/ppermute | solution.py:234
  62.4 5.0 %collective-permute-start.13 = (bf16[384,768]{1,0:T(8,128)(2,1)}, bf16[384,768]{1,0:T(8,128)(2,1)S(1)}, u32[]{:S(2)}, u32[]{:S(2)}) collective-permute-start(bf16[384,768]{1,0:T(8,128)(2,1)} %pack.6.refs_4_), channel_id=1, source_target_pairs={{0,1},{1,2},{2,3},{3,0},{16,19},{17,16},{18,17},{19,18},{32,33},{3... | collective-permute-start | bytes 1769480 | tf_op jit(solution)/shard_map/ppermute | solution.py:234
  67.4 1.5 %collective-permute-done.17.refs_2_ = bf16[512,512]{1,0:T(8,128)(2,1)} collective-permute-done((bf16[512,512]{1,0:T(8,128)(2,1)}, bf16[512,512]{1,0:T(8,128)(2,1)}, u32[]{:S(2)}, u32[]{:S(2)}) %collective-permute-start.17) | collective-permute-done | bytes 524320 | tf_op jit(solution)/shard_map/ppermute | solution.py:234
  69.0 1.5 %order.1.refs_8_ = bf16[2048,512]{1,0:T(8,128)(2,1)S(1)} custom-call(s32[2]{0:T(128)S(1)} %pad_add_fusion.place_ref, bf16[512,512]{1,0:T(8,128)(2,1)S(1)} %pack.7.refs_0_, bf16[512,512]{1,0:T(8,128)(2,1)} %collective-permute-done.16.refs_1_, bf16[512,512]{1,0:T(8,128)(2,1)} %collective-permute-done.17.refs_2_, bf16[512,512]{1,0:T(8,128)(2,1)} %collective-permute-done.18.refs_3_), custom_call_target="tpu_custom_call" | custom-call | tf_op jit(solution)/shard_map/order/pallas_call | solution.py:308
  74.9 5.9 %chunk0.1 = (f32[2048,512]{1,0:T(8,128)}, f32[192,128]{1,0:T(8,128)S(1)}) custom-call(bf16[128,2048]{1,0:T(8,128)(2,1)S(1)} %constant_dynamic-slice_fusion.7.refs_0_, bf16[128,2048]{1,0:T(8,128)(2,1)S(1)} %collective-permute-done.refs_1_.refs_3_, bf16[128,2048]{1,0:T(8,128)(2,1)S(1)} %collective-permute-done.1.refs_3_.refs_2_, ...), custom_call_target="tpu_custom_call" | custom-call | flops 3221225472 | bytes 9437184 | tf_op jit(solution)/shard_map/chunk0/pallas_call | solution.py:133
  80.8 4.2 %chunk3.1 = (f32[2048,512]{1,0:T(8,128)}, f32[128,128]{1,0:T(8,128)S(1)}) custom-call(bf16[128,2048]{1,0:T(8,128)(2,1)S(1)} %constant_dynamic-slice_fusion.7.refs_0_, bf16[128,2048]{1,0:T(8,128)(2,1)S(1)} %collective-permute-done.refs_1_.refs_3_, bf16[128,2048]{1,0:T(8,128)(2,1)S(1)} %collective-permute-done.1.refs_3_.refs_2_, ...), custom_call_target="tpu_custom_call", output_to_operand_aliasing={{0}: (12, {})} | custom-call | flops 2147483648 | bytes 6291456 | tf_op jit(solution)/shard_map/chunk3/pallas_call | solution.py:133
  85.1 4.0 %collective-permute-done.15.refs_6_ = bf16[384,768]{1,0:T(8,128)(2,1)S(1)} collective-permute-done((bf16[384,768]{1,0:T(8,128)(2,1)}, bf16[384,768]{1,0:T(8,128)(2,1)S(1)}, u32[]{:S(2)}, u32[]{:S(2)}) %collective-permute-start.15) | collective-permute-done | bytes 589856 | tf_op jit(solution)/shard_map/ppermute | solution.py:234
  89.0 6.7 %chunk5.1 = (f32[2048,512]{1,0:T(8,128)}, f32[192,128]{1,0:T(8,128)S(1)}) custom-call(bf16[128,2048]{1,0:T(8,128)(2,1)S(1)} %constant_dynamic-slice_fusion.7.refs_0_, bf16[128,2048]{1,0:T(8,128)(2,1)S(1)} %collective-permute-done.refs_1_.refs_3_, bf16[128,2048]{1,0:T(8,128)(2,1)S(1)} %collective-permute-done.1.refs_3_.refs_2_, ...), custom_call_target="tpu_custom_call", output_to_operand_aliasing={{0}: (12, {})} | custom-call | flops 3221225472 | bytes 9437184 | tf_op jit(solution)/shard_map/chunk5/pallas_call | solution.py:133
  96.5 2.7 %collective-permute-start.21 = (f32[256,128]{1,0:T(8,128)S(1)}, f32[256,128]{1,0:T(8,128)S(1)}, u32[]{:S(2)}, u32[]{:S(2)}) collective-permute-start(f32[256,128]{1,0:T(8,128)S(1)} %constant_dynamic-slice_fusion), channel_id=1, source_target_pairs={{0,16},{16,0},{32,48},{48,32},{64,80},{80,64},{96,112},{112,96},{1... | collective-permute-start | bytes 393224 | tf_op jit(solution)/shard_map/ppermute | solution.py:249
  101.1 4.7 %collective-permute-done.22 = f32[256,128]{1,0:T(8,128)S(1)} collective-permute-done((f32[256,128]{1,0:T(8,128)S(1)}, f32[256,128]{1,0:T(8,128)S(1)}, u32[]{:S(2)}, u32[]{:S(2)}) %collective-permute-start.22) | collective-permute-done | bytes 131104 | tf_op jit(solution)/shard_map/ppermute | solution.py:249
  105.9 5.2 %collective-permute-start.23 = (f32[256,128]{1,0:T(8,128)S(1)}, f32[256,128]{1,0:T(8,128)S(1)}, u32[]{:S(2)}, u32[]{:S(2)}) collective-permute-start(f32[256,128]{1,0:T(8,128)S(1)} %add.92), channel_id=1, source_target_pairs={{0,64},{16,208},{32,96},{48,240},{64,0},{80,144},{96,32},{112,176}... | collective-permute-start | bytes 393224 | tf_op jit(solution)/shard_map/ppermute | solution.py:249
  111.1 3.8 %collective-permute-done.23 = f32[256,128]{1,0:T(8,128)S(1)} collective-permute-done((f32[256,128]{1,0:T(8,128)S(1)}, f32[256,128]{1,0:T(8,128)S(1)}, u32[]{:S(2)}, u32[]{:S(2)}) %collective-permute-start.23) | collective-permute-done | bytes 131104 | tf_op jit(solution)/shard_map/ppermute | solution.py:249
  115.7 4.5 %collective-permute-done.24 = f32[256,128]{1,0:T(8,128)S(1)} collective-permute-done((f32[256,128]{1,0:T(8,128)S(1)}, f32[256,128]{1,0:T(8,128)S(1)}, u32[]{:S(2)}, u32[]{:S(2)}) %collective-permute-start.24) | collective-permute-done | bytes 131104 | tf_op jit(solution)/shard_map/ppermute | solution.py:249
  120.2 4.6 %collective-permute-start.25 = (f32[256,128]{1,0:T(8,128)S(1)}, f32[256,128]{1,0:T(8,128)S(1)}, u32[]{:S(2)}, u32[]{:S(2)}) collective-permute-start(f32[256,128]{1,0:T(8,128)S(1)} %add.94), channel_id=1, source_target_pairs={{0,16},{16,0},{32,48},{48,32},{64,80},{80,64},{96,112},{112,96},{1... | collective-permute-start | bytes 393224 | tf_op jit(solution)/shard_map/ppermute | solution.py:249
  125.8 3.0 %spread.1 = bf16[2048,512]{1,0:T(8,128)(2,1)} custom-call(f32[512,128]{1,0:T(8,128)S(1)} %maximum_select_fusion.refs_0_, bf16[640,512]{1,0:T(8,128)(2,1)S(1)} %copy-done.1), custom_call_target="tpu_custom_call" | custom-call | flops 800000000 | bytes 2097152 | tf_op jit(solution)/shard_map/spread/pallas_call | solution.py:172
  (82 shorter events, 18.2 us)
Async XLA Ops:
  1.7 16.3 %collective-permute-start = (bf16[128,2048]{1,0:T(8,128)(2,1)S(1)}, bf16[128,2048]{1,0:T(8,128)(2,1)S(1)}, u32[]{:S(2)}, u32[]{:S(2)}) collective-permute-start(bf16[128,2048]{1,0:T(8,128)(2,1)S(1)} %constant_dynamic-slice_fusion.7.refs_0_), channel_id=1, source_target_pairs={{0,1},{1,2},{2,3},{3,0},{16,19},{17,16},{18,17},{19,18},{32,33},{3... | collective-permute-start | bytes 1572872 | tf_op jit(solution)/shard_map/ppermute | solution.py:234
  4.3 13.8 %collective-permute-start.2 = (bf16[128,2048]{1,0:T(8,128)(2,1)S(1)}, bf16[128,2048]{1,0:T(8,128)(2,1)S(1)}, u32[]{:S(2)}, u32[]{:S(2)}) collective-permute-start(bf16[128,2048]{1,0:T(8,128)(2,1)S(1)} %constant_dynamic-slice_fusion.7.refs_0_), channel_id=1, source_target_pairs={{0,3},{1,0},{2,1},{3,2},{16,17},{17,18},{18,19},{19,16},{32,35},{3... | collective-permute-start | bytes 1572872 | tf_op jit(solution)/shard_map/ppermute | solution.py:234
  5.5 11.5 %collective-permute-start.3 = (bf16[128,768]{1,0:T(8,128)(2,1)S(1)}, bf16[128,768]{1,0:T(8,128)(2,1)S(1)}, u32[]{:S(2)}, u32[]{:S(2)}) collective-permute-start(bf16[128,768]{1,0:T(8,128)(2,1)S(1)} %get-tuple-element.19), channel_id=1, source_target_pairs={{0,4},{4,8},{8,12},{12,0},{16,28},{20,16},{24,20},{28,24},{32,36},... | collective-permute-start | bytes 589832 | tf_op jit(solution)/shard_map/ppermute | solution.py:234
  6.0 11.0 %collective-permute-start.4 = (bf16[128,768]{1,0:T(8,128)(2,1)S(1)}, bf16[128,768]{1,0:T(8,128)(2,1)S(1)}, u32[]{:S(2)}, u32[]{:S(2)}) collective-permute-start(bf16[128,768]{1,0:T(8,128)(2,1)S(1)} %get-tuple-element.18), channel_id=1, source_target_pairs={{0,8},{4,12},{8,0},{12,4},{16,24},{20,28},{24,16},{28,20},{32,40},... | collective-permute-start | bytes 589832 | tf_op jit(solution)/shard_map/ppermute | solution.py:234
  6.7 11.4 %collective-permute-start.5 = (bf16[128,768]{1,0:T(8,128)(2,1)S(1)}, bf16[128,768]{1,0:T(8,128)(2,1)S(1)}, u32[]{:S(2)}, u32[]{:S(2)}) collective-permute-start(bf16[128,768]{1,0:T(8,128)(2,1)S(1)} %get-tuple-element.17), channel_id=1, source_target_pairs={{0,12},{4,0},{8,4},{12,8},{16,20},{20,24},{24,28},{28,16},{32,44},... | collective-permute-start | bytes 589832 | tf_op jit(solution)/shard_map/ppermute | solution.py:234
  19.7 10.9 %collective-permute-start.9 = (bf16[384,768]{1,0:T(8,128)(2,1)S(1)}, bf16[384,768]{1,0:T(8,128)(2,1)S(1)}, u32[]{:S(2)}, u32[]{:S(2)}) collective-permute-start(bf16[384,768]{1,0:T(8,128)(2,1)S(1)} %pack.4.refs_4_), channel_id=1, source_target_pairs={{0,3},{1,0},{2,1},{3,2},{16,17},{17,18},{18,19},{19,16},{32,35},{3... | collective-permute-start | bytes 1769480 | tf_op jit(solution)/shard_map/ppermute | solution.py:234
  21.2 12.1 %copy-start.14 = (bf16[512,512]{1,0:T(8,128)(2,1)S(1)}, bf16[512,512]{1,0:T(8,128)(2,1)}, u32[]{:S(2)}) copy-start(bf16[512,512]{1,0:T(8,128)(2,1)} %refs_0_.1) | copy-start | bytes 1572868
  21.2 7.2 %collective-permute-start.6 = (bf16[128,1280]{1,0:T(8,128)(2,1)S(1)}, bf16[128,1280]{1,0:T(8,128)(2,1)S(1)}, u32[]{:S(2)}, u32[]{:S(2)}) collective-permute-start(bf16[128,1280]{1,0:T(8,128)(2,1)S(1)} %after.3), channel_id=1, source_target_pairs={{0,4},{4,8},{8,12},{12,0},{16,28},{20,16},{24,20},{28,24},{32,36},... | collective-permute-start | bytes 983048 | tf_op jit(solution)/shard_map/ppermute | solution.py:234
  21.9 14.3 %collective-permute-start.11 = (bf16[384,768]{1,0:T(8,128)(2,1)S(1)}, bf16[384,768]{1,0:T(8,128)(2,1)S(1)}, u32[]{:S(2)}, u32[]{:S(2)}) collective-permute-start(bf16[384,768]{1,0:T(8,128)(2,1)S(1)} %pack.4.refs_4_), channel_id=1, source_target_pairs={{0,1},{1,2},{2,3},{3,0},{16,19},{17,16},{18,17},{19,18},{32,33},{3... | collective-permute-start | bytes 1769480 | tf_op jit(solution)/shard_map/ppermute | solution.py:234
  24.5 9.5 %collective-permute-start.8 = (bf16[128,1280]{1,0:T(8,128)(2,1)S(1)}, bf16[128,1280]{1,0:T(8,128)(2,1)S(1)}, u32[]{:S(2)}, u32[]{:S(2)}) collective-permute-start(bf16[128,1280]{1,0:T(8,128)(2,1)S(1)} %after.5), channel_id=1, source_target_pairs={{0,12},{4,0},{8,4},{12,8},{16,20},{20,24},{24,28},{28,16},{32,44},... | collective-permute-start | bytes 983048 | tf_op jit(solution)/shard_map/ppermute | solution.py:234
  28.4 7.8 %collective-permute-start.7 = (bf16[128,1280]{1,0:T(8,128)(2,1)S(1)}, bf16[128,1280]{1,0:T(8,128)(2,1)S(1)}, u32[]{:S(2)}, u32[]{:S(2)}) collective-permute-start(bf16[128,1280]{1,0:T(8,128)(2,1)S(1)} %after.4), channel_id=1, source_target_pairs={{0,8},{4,12},{8,0},{12,4},{16,24},{20,28},{24,16},{28,20},{32,40},... | collective-permute-start | bytes 983048 | tf_op jit(solution)/shard_map/ppermute | solution.py:234
  30.5 23.0 %copy-start.6 = (bf16[384,768]{1,0:T(8,128)(2,1)}, bf16[384,768]{1,0:T(8,128)(2,1)S(1)}, u32[]{:S(2)}) copy-start(bf16[384,768]{1,0:T(8,128)(2,1)S(1)} %collective-permute-done.9.refs_4_.refs_7_) | copy-start | bytes 1769476
  30.5 21.9 %collective-permute-start.10 = (bf16[384,768]{1,0:T(8,128)(2,1)S(1)}, bf16[384,768]{1,0:T(8,128)(2,1)S(1)}, u32[]{:S(2)}, u32[]{:S(2)}) collective-permute-start(bf16[384,768]{1,0:T(8,128)(2,1)S(1)} %collective-permute-done.9.refs_4_.refs_7_), channel_id=1, source_target_pairs={{0,3},{1,0},{2,1},{3,2},{16,17},{17,18},{18,19},{19,16},{32,35},{3... | collective-permute-start | bytes 1769480 | tf_op jit(solution)/shard_map/ppermute | solution.py:234
  30.6 13.8 %collective-permute-start.1 = (bf16[128,2048]{1,0:T(8,128)(2,1)S(1)}, bf16[128,2048]{1,0:T(8,128)(2,1)S(1)}, u32[]{:S(2)}, u32[]{:S(2)}) collective-permute-start(bf16[128,2048]{1,0:T(8,128)(2,1)S(1)} %collective-permute-done.refs_1_.refs_3_), channel_id=1, source_target_pairs={{0,1},{1,2},{2,3},{3,0},{16,19},{17,16},{18,17},{19,18},{32,33},{3... | collective-permute-start | bytes 1572872 | tf_op jit(solution)/shard_map/ppermute | solution.py:234
  34.0 22.4 %collective-permute-start.16 = (bf16[512,512]{1,0:T(8,128)(2,1)S(1)}, bf16[512,512]{1,0:T(8,128)(2,1)}, u32[]{:S(2)}, u32[]{:S(2)}) collective-permute-start(bf16[512,512]{1,0:T(8,128)(2,1)S(1)} %pack.7.refs_0_), channel_id=1, source_target_pairs={{0,4},{4,8},{8,12},{12,0},{16,28},{20,16},{24,20},{28,24},{32,36},... | collective-permute-start | bytes 1572872 | tf_op jit(solution)/shard_map/ppermute | solution.py:234
  36.2 16.3 %copy-start.8 = (bf16[384,768]{1,0:T(8,128)(2,1)}, bf16[384,768]{1,0:T(8,128)(2,1)S(1)}, u32[]{:S(2)}) copy-start(bf16[384,768]{1,0:T(8,128)(2,1)S(1)} %collective-permute-done.11.refs_3_.refs_5_) | copy-start | bytes 1769476
  36.8 7.5 %copy-start.2 = (bf16[384,512]{1,0:T(8,128)(2,1)}, bf16[384,512]{1,0:T(8,128)(2,1)S(1)}, u32[]{:S(2)}) copy-start(bf16[384,512]{1,0:T(8,128)(2,1)S(1)} %pack.5.refs_4_) | copy-start | bytes 1179652
  36.8 15.6 %collective-permute-start.12 = (bf16[384,512]{1,0:T(8,128)(2,1)S(1)}, bf16[384,512]{1,0:T(8,128)(2,1)S(1)}, u32[]{:S(2)}, u32[]{:S(2)}) collective-permute-start(bf16[384,512]{1,0:T(8,128)(2,1)S(1)} %pack.5.refs_4_), channel_id=1, source_target_pairs={{0,1},{1,2},{2,3},{3,0},{16,19},{17,16},{18,17},{19,18},{32,33},{3... | collective-permute-start | bytes 1179656 | tf_op jit(solution)/shard_map/ppermute | solution.py:234
  53.5 17.0 %collective-permute-start.14 = (bf16[384,768]{1,0:T(8,128)(2,1)}, bf16[384,768]{1,0:T(8,128)(2,1)}, u32[]{:S(2)}, u32[]{:S(2)}) collective-permute-start(bf16[384,768]{1,0:T(8,128)(2,1)} %pack.6.refs_4_), channel_id=1, source_target_pairs={{0,3},{1,0},{2,1},{3,2},{16,17},{17,18},{18,19},{19,16},{32,35},{3... | collective-permute-start | bytes 1769480 | tf_op jit(solution)/shard_map/ppermute | solution.py:234
  53.6 8.8 %collective-permute-start.18 = (bf16[512,512]{1,0:T(8,128)(2,1)S(1)}, bf16[512,512]{1,0:T(8,128)(2,1)}, u32[]{:S(2)}, u32[]{:S(2)}) collective-permute-start(bf16[512,512]{1,0:T(8,128)(2,1)S(1)} %pack.7.refs_0_), channel_id=1, source_target_pairs={{0,12},{4,0},{8,4},{12,8},{16,20},{20,24},{24,28},{28,16},{32,44},... | collective-permute-start | bytes 1572872 | tf_op jit(solution)/shard_map/ppermute | solution.py:234
  56.3 12.7 %collective-permute-start.17 = (bf16[512,512]{1,0:T(8,128)(2,1)}, bf16[512,512]{1,0:T(8,128)(2,1)}, u32[]{:S(2)}, u32[]{:S(2)}) collective-permute-start(bf16[512,512]{1,0:T(8,128)(2,1)} %collective-permute-done.16.refs_1_), channel_id=1, source_target_pairs={{0,4},{4,8},{8,12},{12,0},{16,28},{20,16},{24,20},{28,24},{32,36},... | collective-permute-start | bytes 1572872 | tf_op jit(solution)/shard_map/ppermute | solution.py:234
  58.3 12.3 %copy-start.1 = (bf16[640,512]{1,0:T(8,128)(2,1)S(1)}, bf16[640,512]{1,0:T(8,128)(2,1)}, u32[]{:S(2)}) copy-start(bf16[640,512]{1,0:T(8,128)(2,1)} %constant.50.clone.refs_11_.refs_1_) | copy-start | bytes 1966084
  59.1 11.5 %copy-start = (f32[1,2048,512]{2,1,0:T(8,128)S(1)}, f32[1,2048,512]{2,1,0:T(8,128)}, u32[]{:S(2)}) copy-start(f32[1,2048,512]{2,1,0:T(8,128)} %param.8) | copy-start | bytes 12582916
  59.1 21.7 %collective-permute-start.20 = (bf16[384,512]{1,0:T(8,128)(2,1)}, bf16[384,512]{1,0:T(8,128)(2,1)S(1)}, u32[]{:S(2)}, u32[]{:S(2)}) collective-permute-start(bf16[384,512]{1,0:T(8,128)(2,1)} %copy-done.2), channel_id=1, source_target_pairs={{0,3},{1,0},{2,1},{3,2},{16,17},{17,18},{18,19},{19,16},{32,35},{3... | collective-permute-start | bytes 1179656 | tf_op jit(solution)/shard_map/ppermute | solution.py:234
  59.2 21.6 %collective-permute-start.19 = (bf16[384,512]{1,0:T(8,128)(2,1)}, bf16[384,512]{1,0:T(8,128)(2,1)S(1)}, u32[]{:S(2)}, u32[]{:S(2)}) collective-permute-start(bf16[384,512]{1,0:T(8,128)(2,1)} %copy-done.4), channel_id=1, source_target_pairs={{0,1},{1,2},{2,3},{3,0},{16,19},{17,16},{18,17},{19,18},{32,33},{3... | collective-permute-start | bytes 1179656 | tf_op jit(solution)/shard_map/ppermute | solution.py:234
  62.4 22.6 %collective-permute-start.13 = (bf16[384,768]{1,0:T(8,128)(2,1)}, bf16[384,768]{1,0:T(8,128)(2,1)S(1)}, u32[]{:S(2)}, u32[]{:S(2)}) collective-permute-start(bf16[384,768]{1,0:T(8,128)(2,1)} %pack.6.refs_4_), channel_id=1, source_target_pairs={{0,1},{1,2},{2,3},{3,0},{16,19},{17,16},{18,17},{19,18},{32,33},{3... | collective-permute-start | bytes 1769480 | tf_op jit(solution)/shard_map/ppermute | solution.py:234
  70.5 18.5 %collective-permute-start.15 = (bf16[384,768]{1,0:T(8,128)(2,1)}, bf16[384,768]{1,0:T(8,128)(2,1)S(1)}, u32[]{:S(2)}, u32[]{:S(2)}) collective-permute-start(bf16[384,768]{1,0:T(8,128)(2,1)} %collective-permute-done.14.refs_7_), channel_id=1, source_target_pairs={{0,3},{1,0},{2,1},{3,2},{16,17},{17,18},{18,19},{19,16},{32,35},{3... | collective-permute-start | bytes 1769480 | tf_op jit(solution)/shard_map/ppermute | solution.py:234
  96.5 3.7 %collective-permute-start.21 = (f32[256,128]{1,0:T(8,128)S(1)}, f32[256,128]{1,0:T(8,128)S(1)}, u32[]{:S(2)}, u32[]{:S(2)}) collective-permute-start(f32[256,128]{1,0:T(8,128)S(1)} %constant_dynamic-slice_fusion), channel_id=1, source_target_pairs={{0,16},{16,0},{32,48},{48,32},{64,80},{80,64},{96,112},{112,96},{1... | collective-permute-start | bytes 393224 | tf_op jit(solution)/shard_map/ppermute | solution.py:249
  101.0 4.8 %collective-permute-start.22 = (f32[256,128]{1,0:T(8,128)S(1)}, f32[256,128]{1,0:T(8,128)S(1)}, u32[]{:S(2)}, u32[]{:S(2)}) collective-permute-start(f32[256,128]{1,0:T(8,128)S(1)} %dynamic-slice_add_fusion), channel_id=1, source_target_pairs={{0,32},{16,48},{32,0},{48,16},{64,96},{80,112},{96,64},{112,80},{1... | collective-permute-start | bytes 393224 | tf_op jit(solution)/shard_map/ppermute | solution.py:249
  105.9 9.0 %collective-permute-start.23 = (f32[256,128]{1,0:T(8,128)S(1)}, f32[256,128]{1,0:T(8,128)S(1)}, u32[]{:S(2)}, u32[]{:S(2)}) collective-permute-start(f32[256,128]{1,0:T(8,128)S(1)} %add.92), channel_id=1, source_target_pairs={{0,64},{16,208},{32,96},{48,240},{64,0},{80,144},{96,32},{112,176}... | collective-permute-start | bytes 393224 | tf_op jit(solution)/shard_map/ppermute | solution.py:249
  114.9 5.3 %collective-permute-start.24 = (f32[256,128]{1,0:T(8,128)S(1)}, f32[256,128]{1,0:T(8,128)S(1)}, u32[]{:S(2)}, u32[]{:S(2)}) collective-permute-start(f32[256,128]{1,0:T(8,128)S(1)} %add.93), channel_id=1, source_target_pairs={{0,224},{16,112},{32,192},{48,80},{64,160},{80,48},{96,128},{112,1... | collective-permute-start | bytes 393224 | tf_op jit(solution)/shard_map/ppermute | solution.py:249
  120.2 5.6 %collective-permute-start.25 = (f32[256,128]{1,0:T(8,128)S(1)}, f32[256,128]{1,0:T(8,128)S(1)}, u32[]{:S(2)}, u32[]{:S(2)}) collective-permute-start(f32[256,128]{1,0:T(8,128)S(1)} %add.94), channel_id=1, source_target_pairs={{0,16},{16,0},{32,48},{48,32},{64,80},{80,64},{96,112},{112,96},{1... | collective-permute-start | bytes 393224 | tf_op jit(solution)/shard_map/ppermute | solution.py:249
  (12 other events, 31.2 us)
where the time goes:
time: 130 us; the launch traced here: 129 us
  waiting for transfers between devices  50 us (38%)
  starting transfers between devices  41.1 us (32%)
  Pallas kernels  25.4 us (20%)
  local copies, waits for them, and re-layouts  10.4 us (8%)
    ppermute x21, waiting for transfers between devices, apart(): return lax.ppermute(x, ('replica', axis), pairs)  35 us
    ppermute x21, starting transfers between devices, apart(): return lax.ppermute(x, ('replica', axis), pairs)  27.7 us
    pallas_call x3, Pallas kernels, chunk(): pl.pallas_call(chunk_kernel, grid=(steps,), in_specs=in_specs + [HBM] * (...  16.8 us
    ppermute x5, waiting for transfers between devices, swapped(): return lax.ppermute(x, 'replica', pairs)  14.9 us
    ppermute x5, starting transfers between devices, swapped(): return lax.ppermute(x, 'replica', pairs)  13.4 us
    unnamed x38, local copies, waits for them, and re-layouts  6.88 us
    dynamic_slice x3, local copies, waits for them, and re-layouts, columns(): lax.dynamic_slice(activations, (0, owner * rows + start), (activations.sh...  3.48 us
    pallas_call x4, Pallas kernels, pack(): pl.pallas_call(functools.partial(pack_kernel, start=start, places=places)...  3.28 us
  transfers between devices with their start and end apart: 26, of which 16 were waited for; matrix products, arithmetic and copies ran while one was open for 2% of the time, Pallas kernels for 11%

commit v1 on v0

--- a/solution.py
+++ b/solution.py
@@ -249,10 +249,36 @@
     return lax.ppermute(x, "replica", pairs)
 
 
-def over_replicas(x, core):
-    half = x.shape[0] // 2
-    mine = lax.dynamic_slice(x, (core * half, 0), (half, x.shape[1]))
-    theirs = lax.dynamic_slice(x, ((1 - core) * half, 0), (half, x.shape[1]))
+def halve_kernel(core_ref, *refs):
+    parts, mine, theirs = refs[:-2], refs[-2], refs[-1]
+    half, start = mine.shape[0], 0
+    for part in parts:
+        for row in range(0, part.shape[0], 64):
+            upper = (start + row) // half
+            value = part[pl.ds(row, 64), :]
+            here = pl.ds((start + row) % half, 64)
+
+            @pl.when(core_ref[0] == upper)
+            def _():
+                mine[here, :] = value
+
+            @pl.when(core_ref[0] != upper)
+            def _():
+                theirs[here, :] = value
+
+        start += part.shape[0]
+
+
+def over_replicas(parts, core):
+    half = jax.ShapeDtypeStruct((sum(p.shape[0] for p in parts) // 2, parts[0].shape[1]), parts[0].dtype)
+    mine, theirs = pl.pallas_call(
+        halve_kernel,
+        in_specs=[SMEM] + [VMEM] * len(parts),
+        out_specs=[VMEM] * 2,
+        out_shape=[half, half],
+        compiler_params=PARAMS,
+        name="halve",
+    )(core.reshape(1).astype(jnp.int32), *parts)
     mine = mine + swapped(theirs, lambda z, c: (z, 1 - c))
     def quad(z, c):
         return (((z - 2 * c) % 8 ^ 2) + 2 * c) % 8, c
@@ -294,7 +320,7 @@
     late = [late_one, apart(after(pieces[4], late_one), "fsdp", 2), late_three]
     cots = around(pack([cotangent], 0, cols, late_one), "fsdp")
 
-    chunks = [(0, 3), (3, 2), (5, 3)]
+    chunks = [(0, 3), (3, 4), (7, 1)]
     units = [own]
     for first, steps in chunks:
         if first == 0:
@@ -302,7 +328,7 @@
         else:
             before = [units[-1][1], units[-1][3]] if first == 3 else [own[2], units[-2][2], units[-1][1]]
             unit = pack(late, first * TILE - 768, steps * TILE, *before)
-        units.append(around(unit, "tensor", first in (0, 5)))
+        units.append(around(unit, "tensor", first in (0, 7)))
     others = units[1:]
 
     cot = pl.pallas_call(
@@ -331,7 +357,7 @@
     for i in range(len(chunks)):
         new_momentum, kept_i = part(i, new_momentum)
         kept.append(kept_i)
-    combined = over_replicas(jnp.concatenate(kept, 0), core)
+    combined = over_replicas(kept, core)
     update = spread(combined, (rows, cols), table)
     return (new_momentum[None], update)
 

time: 130 us -> 128 us (0.985)
  the two profiles are of different devices: /device:TPU:57 before, /device:TPU:1 now
where the time goes in v1:
time: 128 us; the launch traced here: 126 us
  waiting for transfers between devices  57.8 us (45%)
  starting transfers between devices  33.5 us (26%)
  Pallas kernels  26.1 us (20%)
  local copies, waits for them, and re-layouts  7.6 us (6%)
    ppermute x21, waiting for transfers between devices, apart(): return lax.ppermute(x, ('replica', axis), pairs)  44.8 us
    ppermute x21, starting transfers between devices, apart(): return lax.ppermute(x, ('replica', axis), pairs)  19.4 us
    pallas_call x3, Pallas kernels, chunk(): pl.pallas_call(chunk_kernel, grid=(steps,), in_specs=in_specs + [HBM] * (...  17.6 us
    ppermute x5, starting transfers between devices, swapped(): return lax.ppermute(x, 'replica', pairs)  14.1 us
    ppermute x5, waiting for transfers between devices, swapped(): return lax.ppermute(x, 'replica', pairs)  13.1 us
    unnamed x26, local copies, waits for them, and re-layouts  4.12 us
    dynamic_slice x3, local copies, waits for them, and re-layouts, columns(): lax.dynamic_slice(activations, (0, owner * rows + start), (activations.sh...  3.48 us
    pallas_call x4, Pallas kernels, pack(): pl.pallas_call(functools.partial(pack_kernel, start=start, places=places)...  3.08 us
  transfers between devices with their start and end apart: 26, of which 14 were waited for; matrix products, arithmetic and copies ran while one was open for 2% of the time, Pallas kernels for 15%

profile of v1, /device:TPU:1, one launch (start us, length us, event | category | flops | bytes accessed | tf_op | source)
XLA Modules:
  0.0 126.2 jit_solution(1201920618482822608)
XLA Ops:
  0.6 1.1 constant_dynamic-slice_fusion.6.refs_0_
  1.7 3.4 %collective-permute-start = (bf16[128,2048]{1,0:T(8,128)(2,1)S(1)}, bf16[128,2048]{1,0:T(8,128)(2,1)S(1)}, u32[]{:S(2)}, u32[]{:S(2)}) collective-permute-start(bf16[128,2048]{1,0:T(8,128)(2,1)S(1)} %constant_dynamic-slice_fusion.6.refs_0_), channel_id=1, source_target_pairs={{0,1},{1,2},{2,3},{3,0},{16,19},{17,16},{18,17},{19,18},{32,33},{3... | collective-permute-start | bytes 1572872 | tf_op jit(solution)/shard_map/ppermute | solution.py:234
  5.1 1.2 constant_dynamic-slice_fusion.2
  6.3 2.8 %collective-permute-start.3 = (bf16[128,768]{1,0:T(8,128)(2,1)S(1)}, bf16[128,768]{1,0:T(8,128)(2,1)S(1)}, u32[]{:S(2)}, u32[]{:S(2)}) collective-permute-start(bf16[128,768]{1,0:T(8,128)(2,1)S(1)} %get-tuple-element.23), channel_id=1, source_target_pairs={{0,4},{4,8},{8,12},{12,0},{16,28},{20,16},{24,20},{28,24},{32,36},... | collective-permute-start | bytes 589832 | tf_op jit(solution)/shard_map/ppermute | solution.py:234
  10.1 1.2 constant_dynamic-slice_fusion
  11.4 2.4 %collective-permute-done.3.refs_2_.refs_0_ = bf16[128,768]{1,0:T(8,128)(2,1)S(1)} collective-permute-done((bf16[128,768]{1,0:T(8,128)(2,1)S(1)}, bf16[128,768]{1,0:T(8,128)(2,1)S(1)}, u32[]{:S(2)}, u32[]{:S(2)}) %collective-permute-start.3) | collective-permute-done | bytes 196640 | tf_op jit(solution)/shard_map/ppermute | solution.py:234
  13.8 3.3 %collective-permute-done.4.refs_3_.refs_1_ = bf16[128,768]{1,0:T(8,128)(2,1)S(1)} collective-permute-done((bf16[128,768]{1,0:T(8,128)(2,1)S(1)}, bf16[128,768]{1,0:T(8,128)(2,1)S(1)}, u32[]{:S(2)}, u32[]{:S(2)}) %collective-permute-start.4) | collective-permute-done | bytes 196640 | tf_op jit(solution)/shard_map/ppermute | solution.py:234
  17.1 4.0 %collective-permute-done.5.refs_4_.refs_2_ = bf16[128,768]{1,0:T(8,128)(2,1)S(1)} collective-permute-done((bf16[128,768]{1,0:T(8,128)(2,1)S(1)}, bf16[128,768]{1,0:T(8,128)(2,1)S(1)}, u32[]{:S(2)}, u32[]{:S(2)}) %collective-permute-start.5) | collective-permute-done | bytes 196640 | tf_op jit(solution)/shard_map/ppermute | solution.py:234
  21.6 1.6 %pack.4.refs_4_ = bf16[384,768]{1,0:T(8,128)(2,1)S(1)} custom-call(bf16[128,768]{1,0:T(8,128)(2,1)S(1)} %collective-permute-done.3.refs_2_.refs_0_, bf16[128,768]{1,0:T(8,128)(2,1)S(1)} %collective-permute-done.4.refs_3_.refs_1_, bf16[128,768]{1,0:T(8,128)(2,1)S(1)} %collective-permute-done.5.refs_4_.refs_2_, ...), custom_call_target="tpu_custom_call" | custom-call | tf_op jit(solution)/shard_map/pack/pallas_call | solution.py:202
  23.5 2.5 %collective-permute-start.11 = (bf16[384,768]{1,0:T(8,128)(2,1)S(1)}, bf16[384,768]{1,0:T(8,128)(2,1)S(1)}, u32[]{:S(2)}, u32[]{:S(2)}) collective-permute-start(bf16[384,768]{1,0:T(8,128)(2,1)S(1)} %pack.4.refs_4_), channel_id=1, source_target_pairs={{0,1},{1,2},{2,3},{3,0},{16,19},{17,16},{18,17},{19,18},{32,33},{3... | collective-permute-start | bytes 1769480 | tf_op jit(solution)/shard_map/ppermute | solution.py:234
  28.0 12.3 %collective-permute-done.8.refs_2_ = bf16[128,1280]{1,0:T(8,128)(2,1)S(1)} collective-permute-done((bf16[128,1280]{1,0:T(8,128)(2,1)S(1)}, bf16[128,1280]{1,0:T(8,128)(2,1)S(1)}, u32[]{:S(2)}, u32[]{:S(2)}) %collective-permute-start.8) | collective-permute-done | bytes 327712 | tf_op jit(solution)/shard_map/ppermute | solution.py:234
  40.4 1.1 pack.5.refs_4_
  41.5 1.2 collective-permute-start.12
  44.7 11.1 %collective-permute-done.16.refs_1_ = bf16[512,512]{1,0:T(8,128)(2,1)} collective-permute-done((bf16[512,512]{1,0:T(8,128)(2,1)S(1)}, bf16[512,512]{1,0:T(8,128)(2,1)}, u32[]{:S(2)}, u32[]{:S(2)}) %collective-permute-start.16) | collective-permute-done | bytes 524320 | tf_op jit(solution)/shard_map/ppermute | solution.py:234
  55.8 2.8 %collective-permute-done.18.refs_3_ = bf16[512,512]{1,0:T(8,128)(2,1)S(1)} collective-permute-done((bf16[512,512]{1,0:T(8,128)(2,1)S(1)}, bf16[512,512]{1,0:T(8,128)(2,1)S(1)}, u32[]{:S(2)}, u32[]{:S(2)}) %collective-permute-start.18) | collective-permute-done | bytes 524320 | tf_op jit(solution)/shard_map/ppermute | solution.py:234
  59.4 2.7 %collective-permute-start.19 = (bf16[384,1024]{1,0:T(8,128)(2,1)}, bf16[384,1024]{1,0:T(8,128)(2,1)}, u32[]{:S(2)}, u32[]{:S(2)}) collective-permute-start(bf16[384,1024]{1,0:T(8,128)(2,1)} %collective-permute-done.12.refs_5_), channel_id=1, source_target_pairs={{0,1},{1,2},{2,3},{3,0},{16,19},{17,16},{18,17},{19,18},{32,33},{3... | collective-permute-start | bytes 2359304 | tf_op jit(solution)/shard_map/ppermute | solution.py:234
  62.1 1.0 copy-done.11
  65.4 1.5 %order.1.refs_8_ = bf16[2048,512]{1,0:T(8,128)(2,1)S(1)} custom-call(s32[2]{0:T(128)S(1)} %pad_add_fusion.place_ref, bf16[512,512]{1,0:T(8,128)(2,1)S(1)} %pack.7.refs_0_, bf16[512,512]{1,0:T(8,128)(2,1)} %collective-permute-done.16.refs_1_, bf16[512,512]{1,0:T(8,128)(2,1)} %collective-permute-done.17.refs_2_, bf16[512,512]{1,0:T(8,128)(2,1)S(1)} %copy-done.9), custom_call_target="tpu_custom_call" | custom-call | tf_op jit(solution)/shard_map/order/pallas_call | solution.py:334
  68.7 6.7 %chunk0.1 = (f32[2048,512]{1,0:T(8,128)}, f32[192,128]{1,0:T(8,128)S(1)}) custom-call(bf16[128,2048]{1,0:T(8,128)(2,1)S(1)} %constant_dynamic-slice_fusion.6.refs_0_, bf16[128,2048]{1,0:T(8,128)(2,1)S(1)} %collective-permute-done.refs_1_.refs_3_, bf16[128,2048]{1,0:T(8,128)(2,1)S(1)} %collective-permute-done.1.refs_3_.refs_2_, ...), custom_call_target="tpu_custom_call" | custom-call | flops 3221225472 | bytes 9437184 | tf_op jit(solution)/shard_map/chunk0/pallas_call | solution.py:133
  75.4 1.5 %collective-permute-start.13 = (bf16[384,256]{1,0:T(8,128)(2,1)S(1)}, bf16[384,256]{1,0:T(8,128)(2,1)S(1)}, u32[]{:S(2)}, u32[]{:S(2)}) collective-permute-start(bf16[384,256]{1,0:T(8,128)(2,1)S(1)} %pack.6.refs_4_), channel_id=1, source_target_pairs={{0,1},{1,2},{2,3},{3,0},{16,19},{17,16},{18,17},{19,18},{32,33},{3... | collective-permute-start | bytes 589832 | tf_op jit(solution)/shard_map/ppermute | solution.py:234
  76.9 7.8 %collective-permute-done.14.refs_7_ = bf16[384,256]{1,0:T(8,128)(2,1)S(1)} collective-permute-done((bf16[384,256]{1,0:T(8,128)(2,1)S(1)}, bf16[384,256]{1,0:T(8,128)(2,1)S(1)}, u32[]{:S(2)}, u32[]{:S(2)}) %collective-permute-start.14) | collective-permute-done | bytes 196640 | tf_op jit(solution)/shard_map/ppermute | solution.py:234
  84.7 8.6 %chunk3.1 = (f32[2048,512]{1,0:T(8,128)}, f32[256,128]{1,0:T(8,128)S(1)}) custom-call(bf16[128,2048]{1,0:T(8,128)(2,1)S(1)} %constant_dynamic-slice_fusion.6.refs_0_, bf16[128,2048]{1,0:T(8,128)(2,1)S(1)} %collective-permute-done.refs_1_.refs_3_, bf16[128,2048]{1,0:T(8,128)(2,1)S(1)} %collective-permute-done.1.refs_3_.refs_2_, ...), custom_call_target="tpu_custom_call", output_to_operand_aliasing={{0}: (12, {})} | custom-call | flops 4294967296 | bytes 12582912 | tf_op jit(solution)/shard_map/chunk3/pallas_call | solution.py:133
  93.3 2.4 %chunk7.1 = (f32[2048,512]{1,0:T(8,128)}, f32[64,128]{1,0:T(8,128)S(1)}) custom-call(bf16[128,2048]{1,0:T(8,128)(2,1)S(1)} %constant_dynamic-slice_fusion.6.refs_0_, bf16[128,2048]{1,0:T(8,128)(2,1)S(1)} %collective-permute-done.refs_1_.refs_3_, bf16[128,2048]{1,0:T(8,128)(2,1)S(1)} %collective-permute-done.1.refs_3_.refs_2_, ...), custom_call_target="tpu_custom_call", output_to_operand_aliasing={{0}: (12, {})} | custom-call | flops 1073741824 | bytes 3145728 | tf_op jit(solution)/shard_map/chunk7/pallas_call | solution.py:133
  95.8 4.3 %collective-permute-start.21 = (f32[256,128]{1,0:T(8,128)S(1)}, f32[256,128]{1,0:T(8,128)S(1)}, u32[]{:S(2)}, u32[]{:S(2)}) collective-permute-start(f32[256,128]{1,0:T(8,128)S(1)} %get-tuple-element.17), channel_id=1, source_target_pairs={{0,16},{16,0},{32,48},{48,32},{64,80},{80,64},{96,112},{112,96},{1... | collective-permute-start | bytes 393224 | tf_op jit(solution)/shard_map/ppermute | solution.py:249
  101.1 1.3 %collective-permute-start.22 = (f32[256,128]{1,0:T(8,128)S(1)}, f32[256,128]{1,0:T(8,128)S(1)}, u32[]{:S(2)}, u32[]{:S(2)}) collective-permute-start(f32[256,128]{1,0:T(8,128)S(1)} %add.83), channel_id=1, source_target_pairs={{0,32},{16,48},{32,0},{48,16},{64,96},{80,112},{96,64},{112,80},{1... | collective-permute-start | bytes 393224 | tf_op jit(solution)/shard_map/ppermute | solution.py:249
  102.4 3.5 %collective-permute-done.22 = f32[256,128]{1,0:T(8,128)S(1)} collective-permute-done((f32[256,128]{1,0:T(8,128)S(1)}, f32[256,128]{1,0:T(8,128)S(1)}, u32[]{:S(2)}, u32[]{:S(2)}) %collective-permute-start.22) | collective-permute-done | bytes 131104 | tf_op jit(solution)/shard_map/ppermute | solution.py:249
  105.9 5.7 %collective-permute-start.23 = (f32[256,128]{1,0:T(8,128)S(1)}, f32[256,128]{1,0:T(8,128)S(1)}, u32[]{:S(2)}, u32[]{:S(2)}) collective-permute-start(f32[256,128]{1,0:T(8,128)S(1)} %add.84), channel_id=1, source_target_pairs={{0,64},{16,208},{32,96},{48,240},{64,0},{80,144},{96,32},{112,176}... | collective-permute-start | bytes 393224 | tf_op jit(solution)/shard_map/ppermute | solution.py:249
  111.6 3.3 %collective-permute-done.23 = f32[256,128]{1,0:T(8,128)S(1)} collective-permute-done((f32[256,128]{1,0:T(8,128)S(1)}, f32[256,128]{1,0:T(8,128)S(1)}, u32[]{:S(2)}, u32[]{:S(2)}) %collective-permute-start.23) | collective-permute-done | bytes 131104 | tf_op jit(solution)/shard_map/ppermute | solution.py:249
  114.9 1.5 %collective-permute-start.24 = (f32[256,128]{1,0:T(8,128)S(1)}, f32[256,128]{1,0:T(8,128)S(1)}, u32[]{:S(2)}, u32[]{:S(2)}) collective-permute-start(f32[256,128]{1,0:T(8,128)S(1)} %add.85), channel_id=1, source_target_pairs={{0,224},{16,112},{32,192},{48,80},{64,160},{80,48},{96,128},{112,1... | collective-permute-start | bytes 393224 | tf_op jit(solution)/shard_map/ppermute | solution.py:249
  116.4 4.3 %collective-permute-done.24 = f32[256,128]{1,0:T(8,128)S(1)} collective-permute-done((f32[256,128]{1,0:T(8,128)S(1)}, f32[256,128]{1,0:T(8,128)S(1)}, u32[]{:S(2)}, u32[]{:S(2)}) %collective-permute-start.24) | collective-permute-done | bytes 131104 | tf_op jit(solution)/shard_map/ppermute | solution.py:249
  120.8 1.2 collective-permute-start.25
  123.0 3.0 %spread.1 = bf16[2048,512]{1,0:T(8,128)(2,1)} custom-call(f32[512,128]{1,0:T(8,128)S(1)} %maximum_select_fusion.refs_0_, bf16[640,512]{1,0:T(8,128)(2,1)S(1)} %copy-done.1), custom_call_target="tpu_custom_call" | custom-call | flops 800000000 | bytes 2097152 | tf_op jit(solution)/shard_map/spread/pallas_call | solution.py:172
  (69 shorter events, 12.8 us)
Async XLA Ops:
  1.7 19.4 %collective-permute-start = (bf16[128,2048]{1,0:T(8,128)(2,1)S(1)}, bf16[128,2048]{1,0:T(8,128)(2,1)S(1)}, u32[]{:S(2)}, u32[]{:S(2)}) collective-permute-start(bf16[128,2048]{1,0:T(8,128)(2,1)S(1)} %constant_dynamic-slice_fusion.6.refs_0_), channel_id=1, source_target_pairs={{0,1},{1,2},{2,3},{3,0},{16,19},{17,16},{18,17},{19,18},{32,33},{3... | collective-permute-start | bytes 1572872 | tf_op jit(solution)/shard_map/ppermute | solution.py:234
  5.1 16.5 %collective-permute-start.2 = (bf16[128,2048]{1,0:T(8,128)(2,1)S(1)}, bf16[128,2048]{1,0:T(8,128)(2,1)S(1)}, u32[]{:S(2)}, u32[]{:S(2)}) collective-permute-start(bf16[128,2048]{1,0:T(8,128)(2,1)S(1)} %constant_dynamic-slice_fusion.6.refs_0_), channel_id=1, source_target_pairs={{0,3},{1,0},{2,1},{3,2},{16,17},{17,18},{18,19},{19,16},{32,35},{3... | collective-permute-start | bytes 1572872 | tf_op jit(solution)/shard_map/ppermute | solution.py:234
  6.3 7.5 %collective-permute-start.3 = (bf16[128,768]{1,0:T(8,128)(2,1)S(1)}, bf16[128,768]{1,0:T(8,128)(2,1)S(1)}, u32[]{:S(2)}, u32[]{:S(2)}) collective-permute-start(bf16[128,768]{1,0:T(8,128)(2,1)S(1)} %get-tuple-element.23), channel_id=1, source_target_pairs={{0,4},{4,8},{8,12},{12,0},{16,28},{20,16},{24,20},{28,24},{32,36},... | collective-permute-start | bytes 589832 | tf_op jit(solution)/shard_map/ppermute | solution.py:234
  9.1 8.0 %collective-permute-start.4 = (bf16[128,768]{1,0:T(8,128)(2,1)S(1)}, bf16[128,768]{1,0:T(8,128)(2,1)S(1)}, u32[]{:S(2)}, u32[]{:S(2)}) collective-permute-start(bf16[128,768]{1,0:T(8,128)(2,1)S(1)} %get-tuple-element.22), channel_id=1, source_target_pairs={{0,8},{4,12},{8,0},{12,4},{16,24},{20,28},{24,16},{28,20},{32,40},... | collective-permute-start | bytes 589832 | tf_op jit(solution)/shard_map/ppermute | solution.py:234
  9.4 11.7 %collective-permute-start.5 = (bf16[128,768]{1,0:T(8,128)(2,1)S(1)}, bf16[128,768]{1,0:T(8,128)(2,1)S(1)}, u32[]{:S(2)}, u32[]{:S(2)}) collective-permute-start(bf16[128,768]{1,0:T(8,128)(2,1)S(1)} %get-tuple-element.21), channel_id=1, source_target_pairs={{0,12},{4,0},{8,4},{12,8},{16,20},{20,24},{24,28},{28,16},{32,44},... | collective-permute-start | bytes 589832 | tf_op jit(solution)/shard_map/ppermute | solution.py:234
  21.1 6.3 %collective-permute-start.6 = (bf16[128,1280]{1,0:T(8,128)(2,1)S(1)}, bf16[128,1280]{1,0:T(8,128)(2,1)S(1)}, u32[]{:S(2)}, u32[]{:S(2)}) collective-permute-start(bf16[128,1280]{1,0:T(8,128)(2,1)S(1)} %after.3), channel_id=1, source_target_pairs={{0,4},{4,8},{8,12},{12,0},{16,28},{20,16},{24,20},{28,24},{32,36},... | collective-permute-start | bytes 983048 | tf_op jit(solution)/shard_map/ppermute | solution.py:234
  23.2 17.2 %copy-start.4 = (bf16[384,768]{1,0:T(8,128)(2,1)}, bf16[384,768]{1,0:T(8,128)(2,1)S(1)}, u32[]{:S(2)}) copy-start(bf16[384,768]{1,0:T(8,128)(2,1)S(1)} %pack.4.refs_4_) | copy-start | bytes 1769476
  23.2 17.1 %collective-permute-start.9 = (bf16[384,768]{1,0:T(8,128)(2,1)S(1)}, bf16[384,768]{1,0:T(8,128)(2,1)}, u32[]{:S(2)}, u32[]{:S(2)}) collective-permute-start(bf16[384,768]{1,0:T(8,128)(2,1)S(1)} %pack.4.refs_4_), channel_id=1, source_target_pairs={{0,3},{1,0},{2,1},{3,2},{16,17},{17,18},{18,19},{19,16},{32,35},{3... | collective-permute-start | bytes 1769480 | tf_op jit(solution)/shard_map/ppermute | solution.py:234
  23.5 16.9 %collective-permute-start.11 = (bf16[384,768]{1,0:T(8,128)(2,1)S(1)}, bf16[384,768]{1,0:T(8,128)(2,1)S(1)}, u32[]{:S(2)}, u32[]{:S(2)}) collective-permute-start(bf16[384,768]{1,0:T(8,128)(2,1)S(1)} %pack.4.refs_4_), channel_id=1, source_target_pairs={{0,1},{1,2},{2,3},{3,0},{16,19},{17,16},{18,17},{19,18},{32,33},{3... | collective-permute-start | bytes 1769480 | tf_op jit(solution)/shard_map/ppermute | solution.py:234
  26.0 16.8 %copy-start.10 = (bf16[512,512]{1,0:T(8,128)(2,1)S(1)}, bf16[512,512]{1,0:T(8,128)(2,1)}, u32[]{:S(2)}) copy-start(bf16[512,512]{1,0:T(8,128)(2,1)} %refs_0_.1) | copy-start | bytes 1572868
  26.0 14.4 %collective-permute-start.8 = (bf16[128,1280]{1,0:T(8,128)(2,1)S(1)}, bf16[128,1280]{1,0:T(8,128)(2,1)S(1)}, u32[]{:S(2)}, u32[]{:S(2)}) collective-permute-start(bf16[128,1280]{1,0:T(8,128)(2,1)S(1)} %after.5), channel_id=1, source_target_pairs={{0,12},{4,0},{8,4},{12,8},{16,20},{20,24},{24,28},{28,16},{32,44},... | collective-permute-start | bytes 983048 | tf_op jit(solution)/shard_map/ppermute | solution.py:234
  27.5 34.6 %copy-start.12 = (s32[1,32,8,16]{1,3,2,0:T(8,128)S(1)}, s32[1,32,8,16]{1,3,2,0:T(8,128)}, u32[]{:S(2)}) copy-start(s32[1,32,8,16]{1,3,2,0:T(8,128)} %param.9) | copy-start | bytes 49156
  27.5 12.9 %collective-permute-start.7 = (bf16[128,1280]{1,0:T(8,128)(2,1)S(1)}, bf16[128,1280]{1,0:T(8,128)(2,1)S(1)}, u32[]{:S(2)}, u32[]{:S(2)}) collective-permute-start(bf16[128,1280]{1,0:T(8,128)(2,1)S(1)} %after.4), channel_id=1, source_target_pairs={{0,8},{4,12},{8,0},{12,4},{16,24},{20,28},{24,16},{28,20},{32,40},... | collective-permute-start | bytes 983048 | tf_op jit(solution)/shard_map/ppermute | solution.py:234
  40.4 2.5 %copy-start.6 = (bf16[384,768]{1,0:T(8,128)(2,1)}, bf16[384,768]{1,0:T(8,128)(2,1)S(1)}, u32[]{:S(2)}) copy-start(bf16[384,768]{1,0:T(8,128)(2,1)S(1)} %collective-permute-done.11.refs_3_.refs_5_) | copy-start | bytes 1769476
  41.5 17.9 %collective-permute-start.12 = (bf16[384,1024]{1,0:T(8,128)(2,1)}, bf16[384,1024]{1,0:T(8,128)(2,1)}, u32[]{:S(2)}, u32[]{:S(2)}) collective-permute-start(bf16[384,1024]{1,0:T(8,128)(2,1)} %pack.5.refs_4_), channel_id=1, source_target_pairs={{0,1},{1,2},{2,3},{3,0},{16,19},{17,16},{18,17},{19,18},{32,33},{3... | collective-permute-start | bytes 2359304 | tf_op jit(solution)/shard_map/ppermute | solution.py:234
  42.8 12.9 %collective-permute-start.16 = (bf16[512,512]{1,0:T(8,128)(2,1)S(1)}, bf16[512,512]{1,0:T(8,128)(2,1)}, u32[]{:S(2)}, u32[]{:S(2)}) collective-permute-start(bf16[512,512]{1,0:T(8,128)(2,1)S(1)} %pack.7.refs_0_), channel_id=1, source_target_pairs={{0,4},{4,8},{8,12},{12,0},{16,28},{20,16},{24,20},{28,24},{32,36},... | collective-permute-start | bytes 1572872 | tf_op jit(solution)/shard_map/ppermute | solution.py:234
  43.5 15.1 %collective-permute-start.18 = (bf16[512,512]{1,0:T(8,128)(2,1)S(1)}, bf16[512,512]{1,0:T(8,128)(2,1)S(1)}, u32[]{:S(2)}, u32[]{:S(2)}) collective-permute-start(bf16[512,512]{1,0:T(8,128)(2,1)S(1)} %pack.7.refs_0_), channel_id=1, source_target_pairs={{0,12},{4,0},{8,4},{12,8},{16,20},{20,24},{24,28},{28,16},{32,44},... | collective-permute-start | bytes 1572872 | tf_op jit(solution)/shard_map/ppermute | solution.py:234
  44.4 22.6 %collective-permute-start.10 = (bf16[384,768]{1,0:T(8,128)(2,1)}, bf16[384,768]{1,0:T(8,128)(2,1)}, u32[]{:S(2)}, u32[]{:S(2)}) collective-permute-start(bf16[384,768]{1,0:T(8,128)(2,1)} %collective-permute-done.9.refs_4_.refs_7_), channel_id=1, source_target_pairs={{0,3},{1,0},{2,1},{3,2},{16,17},{17,18},{18,19},{19,16},{32,35},{3... | collective-permute-start | bytes 1769480 | tf_op jit(solution)/shard_map/ppermute | solution.py:234
  55.8 8.6 %collective-permute-start.17 = (bf16[512,512]{1,0:T(8,128)(2,1)}, bf16[512,512]{1,0:T(8,128)(2,1)}, u32[]{:S(2)}, u32[]{:S(2)}) collective-permute-start(bf16[512,512]{1,0:T(8,128)(2,1)} %collective-permute-done.16.refs_1_), channel_id=1, source_target_pairs={{0,4},{4,8},{8,12},{12,0},{16,28},{20,16},{24,20},{28,24},{32,36},... | collective-permute-start | bytes 1572872 | tf_op jit(solution)/shard_map/ppermute | solution.py:234
  55.8 11.2 %collective-permute-start.1 = (bf16[128,2048]{1,0:T(8,128)(2,1)S(1)}, bf16[128,2048]{1,0:T(8,128)(2,1)S(1)}, u32[]{:S(2)}, u32[]{:S(2)}) collective-permute-start(bf16[128,2048]{1,0:T(8,128)(2,1)S(1)} %collective-permute-done.refs_1_.refs_3_), channel_id=1, source_target_pairs={{0,1},{1,2},{2,3},{3,0},{16,19},{17,16},{18,17},{19,18},{32,33},{3... | collective-permute-start | bytes 1572872 | tf_op jit(solution)/shard_map/ppermute | solution.py:234
  59.4 25.3 %collective-permute-start.20 = (bf16[384,1024]{1,0:T(8,128)(2,1)}, bf16[384,1024]{1,0:T(8,128)(2,1)}, u32[]{:S(2)}, u32[]{:S(2)}) collective-permute-start(bf16[384,1024]{1,0:T(8,128)(2,1)} %pack.5.refs_4_), channel_id=1, source_target_pairs={{0,3},{1,0},{2,1},{3,2},{16,17},{17,18},{18,19},{19,16},{32,35},{3... | collective-permute-start | bytes 2359304 | tf_op jit(solution)/shard_map/ppermute | solution.py:234
  59.4 25.3 %collective-permute-start.19 = (bf16[384,1024]{1,0:T(8,128)(2,1)}, bf16[384,1024]{1,0:T(8,128)(2,1)}, u32[]{:S(2)}, u32[]{:S(2)}) collective-permute-start(bf16[384,1024]{1,0:T(8,128)(2,1)} %collective-permute-done.12.refs_5_), channel_id=1, source_target_pairs={{0,1},{1,2},{2,3},{3,0},{16,19},{17,16},{18,17},{19,18},{32,33},{3... | collective-permute-start | bytes 2359304 | tf_op jit(solution)/shard_map/ppermute | solution.py:234
  64.0 3.1 %copy-start.3 = (bf16[128,1280]{1,0:T(8,128)(2,1)S(1)}, bf16[128,1280]{1,0:T(8,128)(2,1)}, u32[]{:S(2)}) copy-start(bf16[128,1280]{1,0:T(8,128)(2,1)} %copy-done.2) | copy-start | bytes 983044
  65.4 2.5 %copy-start = (f32[1,2048,512]{2,1,0:T(8,128)S(1)}, f32[1,2048,512]{2,1,0:T(8,128)}, u32[]{:S(2)}) copy-start(f32[1,2048,512]{2,1,0:T(8,128)} %param.8) | copy-start | bytes 12582916
  67.4 17.3 %collective-permute-start.14 = (bf16[384,256]{1,0:T(8,128)(2,1)S(1)}, bf16[384,256]{1,0:T(8,128)(2,1)S(1)}, u32[]{:S(2)}, u32[]{:S(2)}) collective-permute-start(bf16[384,256]{1,0:T(8,128)(2,1)S(1)} %pack.6.refs_4_), channel_id=1, source_target_pairs={{0,3},{1,0},{2,1},{3,2},{16,17},{17,18},{18,19},{19,16},{32,35},{3... | collective-permute-start | bytes 589832 | tf_op jit(solution)/shard_map/ppermute | solution.py:234
  75.4 17.9 %collective-permute-start.13 = (bf16[384,256]{1,0:T(8,128)(2,1)S(1)}, bf16[384,256]{1,0:T(8,128)(2,1)S(1)}, u32[]{:S(2)}, u32[]{:S(2)}) collective-permute-start(bf16[384,256]{1,0:T(8,128)(2,1)S(1)} %pack.6.refs_4_), channel_id=1, source_target_pairs={{0,1},{1,2},{2,3},{3,0},{16,19},{17,16},{18,17},{19,18},{32,33},{3... | collective-permute-start | bytes 589832 | tf_op jit(solution)/shard_map/ppermute | solution.py:234
  84.7 8.6 %collective-permute-start.15 = (bf16[384,256]{1,0:T(8,128)(2,1)S(1)}, bf16[384,256]{1,0:T(8,128)(2,1)S(1)}, u32[]{:S(2)}, u32[]{:S(2)}) collective-permute-start(bf16[384,256]{1,0:T(8,128)(2,1)S(1)} %collective-permute-done.14.refs_7_), channel_id=1, source_target_pairs={{0,3},{1,0},{2,1},{3,2},{16,17},{17,18},{18,19},{19,16},{32,35},{3... | collective-permute-start | bytes 589832 | tf_op jit(solution)/shard_map/ppermute | solution.py:234
  95.8 5.3 %collective-permute-start.21 = (f32[256,128]{1,0:T(8,128)S(1)}, f32[256,128]{1,0:T(8,128)S(1)}, u32[]{:S(2)}, u32[]{:S(2)}) collective-permute-start(f32[256,128]{1,0:T(8,128)S(1)} %get-tuple-element.17), channel_id=1, source_target_pairs={{0,16},{16,0},{32,48},{48,32},{64,80},{80,64},{96,112},{112,96},{1... | collective-permute-start | bytes 393224 | tf_op jit(solution)/shard_map/ppermute | solution.py:249
  101.1 4.8 %collective-permute-start.22 = (f32[256,128]{1,0:T(8,128)S(1)}, f32[256,128]{1,0:T(8,128)S(1)}, u32[]{:S(2)}, u32[]{:S(2)}) collective-permute-start(f32[256,128]{1,0:T(8,128)S(1)} %add.83), channel_id=1, source_target_pairs={{0,32},{16,48},{32,0},{48,16},{64,96},{80,112},{96,64},{112,80},{1... | collective-permute-start | bytes 393224 | tf_op jit(solution)/shard_map/ppermute | solution.py:249
  105.9 9.0 %collective-permute-start.23 = (f32[256,128]{1,0:T(8,128)S(1)}, f32[256,128]{1,0:T(8,128)S(1)}, u32[]{:S(2)}, u32[]{:S(2)}) collective-permute-start(f32[256,128]{1,0:T(8,128)S(1)} %add.84), channel_id=1, source_target_pairs={{0,64},{16,208},{32,96},{48,240},{64,0},{80,144},{96,32},{112,176}... | collective-permute-start | bytes 393224 | tf_op jit(solution)/shard_map/ppermute | solution.py:249
  114.9 5.8 %collective-permute-start.24 = (f32[256,128]{1,0:T(8,128)S(1)}, f32[256,128]{1,0:T(8,128)S(1)}, u32[]{:S(2)}, u32[]{:S(2)}) collective-permute-start(f32[256,128]{1,0:T(8,128)S(1)} %add.85), channel_id=1, source_target_pairs={{0,224},{16,112},{32,192},{48,80},{64,160},{80,48},{96,128},{112,1... | collective-permute-start | bytes 393224 | tf_op jit(solution)/shard_map/ppermute | solution.py:249
  120.8 2.2 %collective-permute-start.25 = (f32[256,128]{1,0:T(8,128)S(1)}, f32[256,128]{1,0:T(8,128)S(1)}, u32[]{:S(2)}, u32[]{:S(2)}) collective-permute-start(f32[256,128]{1,0:T(8,128)S(1)} %add.86), channel_id=1, source_target_pairs={{0,16},{16,0},{32,48},{48,32},{64,80},{80,64},{96,112},{112,96},{1... | collective-permute-start | bytes 393224 | tf_op jit(solution)/shard_map/ppermute | solution.py:249
  (7 other events, 9.9 us)

commit v2 on v1

--- a/solution.py
+++ b/solution.py
@@ -313,21 +313,21 @@
 
     mine = columns(0, 0, rows)
     own = around(mine, "tensor")
-    pieces = [columns(d, 0, 768) for d in (1, 2, 3)] + [columns(d, 768, 1280) for d in (1, 2, 3)]
+    pieces = [columns(d, 0, 1024) for d in (1, 2, 3)] + [columns(d, 1024, 1024) for d in (1, 2, 3)]
     early = [apart(pieces[d - 1], "fsdp", d) for d in (1, 2, 3)]
     late_one = apart(after(pieces[3], own[1], *early), "fsdp", 1)
     late_three = apart(after(pieces[5], own[1], *early), "fsdp", 3)
     late = [late_one, apart(after(pieces[4], late_one), "fsdp", 2), late_three]
     cots = around(pack([cotangent], 0, cols, late_one), "fsdp")
 
-    chunks = [(0, 3), (3, 4), (7, 1)]
+    chunks = [(0, 4), (4, 3), (7, 1)]
     units = [own]
     for first, steps in chunks:
         if first == 0:
-            unit = pack(early, 0, 768, own[1], own[3])
+            unit = pack(early, 0, 1024, own[1], own[3])
         else:
-            before = [units[-1][1], units[-1][3]] if first == 3 else [own[2], units[-2][2], units[-1][1]]
-            unit = pack(late, first * TILE - 768, steps * TILE, *before)
+            before = [units[-1][1], units[-1][3]] if first == 4 else [own[2], units[-2][2], units[-1][1]]
+            unit = pack(late, first * TILE - 1024, steps * TILE, *before)
         units.append(around(unit, "tensor", first in (0, 7)))
     others = units[1:]
 

time: 128 us -> 126 us (0.984)
  starting transfers between devices: 33.5 us -> 38.8 us
  waiting for transfers between devices: 57.8 us -> 54.1 us
  local copies, waits for them, and re-layouts: 7.6 us -> 5.54 us
  Pallas kernels: 26.1 us -> 24.8 us
    ppermute x21, starting transfers between devices: 19.4 us -> 23.2 us  [apart(): return lax.ppermute(x, ('replica', axis), pairs)]
    ppermute x21, waiting for transfers between devices: 44.8 us -> 41.2 us  [apart(): return lax.ppermute(x, ('replica', axis), pairs)]
    ppermute x5, starting transfers between devices: 14.1 us -> 15.6 us  [swapped(): return lax.ppermute(x, 'replica', pairs)]
    pallas_call x4, Pallas kernels: 3.08 us -> 1.67 us  [pack(): pl.pallas_call(functools.partial(pack_kernel, start=start, places=places)...]
    unnamed x26 -> x22, local copies, waits for them, and re-layouts: 4.12 us -> 2.92 us
    dynamic_slice x3 -> x2, local copies, waits for them, and re-layouts: 3.48 us -> 2.62 us  [columns(): lax.dynamic_slice(activations, (0, owner * rows + start), (activations.sh...]
  transfers between devices with their start and end apart: 26 -> 26, of which waited for: 14 -> 13; matrix products, arithmetic and copies ran while one was open for 2% -> 1% of each run, Pallas kernels for 15% -> 15%
where the time goes in v2:
time: 126 us; the launch traced here: 124 us
  waiting for transfers between devices  54.1 us (43%)
  starting transfers between devices  38.8 us (31%)
  Pallas kernels  24.8 us (20%)
  local copies, waits for them, and re-layouts  5.54 us (4%)
    ppermute x21, waiting for transfers between devices, apart(): return lax.ppermute(x, ('replica', axis), pairs)  41.2 us
    ppermute x21, starting transfers between devices, apart(): return lax.ppermute(x, ('replica', axis), pairs)  23.2 us
    pallas_call x3, Pallas kernels, chunk(): pl.pallas_call(chunk_kernel, grid=(steps,), in_specs=in_specs + [HBM] * (...  17.7 us
    ppermute x5, starting transfers between devices, swapped(): return lax.ppermute(x, 'replica', pairs)  15.6 us
    ppermute x5, waiting for transfers between devices, swapped(): return lax.ppermute(x, 'replica', pairs)  12.9 us
    pallas_call x1, Pallas kernels, spread(): pl.pallas_call(lambda *refs: spread_kernel(0, steps, *refs), in_specs=[VM...  3.04 us
    unnamed x22, local copies, waits for them, and re-layouts  2.92 us
    dynamic_slice x2, local copies, waits for them, and re-layouts, columns(): lax.dynamic_slice(activations, (0, owner * rows + start), (activations.sh...  2.62 us
  transfers between devices with their start and end apart: 26, of which 13 were waited for; matrix products, arithmetic and copies ran while one was open for 1% of the time, Pallas kernels for 15%

profile of v2, /device:TPU:1, one launch (start us, length us, event | category | flops | bytes accessed | tf_op | source)
XLA Modules:
  0.0 124.4 jit_solution(9203678179655757435)
XLA Ops:
  0.6 1.1 constant_dynamic-slice_fusion.6.refs_0_
  1.7 3.4 %collective-permute-start = (bf16[128,2048]{1,0:T(8,128)(2,1)S(1)}, bf16[128,2048]{1,0:T(8,128)(2,1)S(1)}, u32[]{:S(2)}, u32[]{:S(2)}) collective-permute-start(bf16[128,2048]{1,0:T(8,128)(2,1)S(1)} %constant_dynamic-slice_fusion.6.refs_0_), channel_id=1, source_target_pairs={{0,1},{1,2},{2,3},{3,0},{16,19},{17,16},{18,17},{19,18},{32,33},{3... | collective-permute-start | bytes 1572872 | tf_op jit(solution)/shard_map/ppermute | solution.py:234
  5.1 1.5 %constant_dynamic-slice_fusion = (bf16[128,1024]{1,0:T(8,128)(2,1)S(1)}, bf16[128,1024]{1,0:T(8,128)(2,1)S(1)}, bf16[128,1024]{1,0:T(8,128)(2,1)S(1)}, bf16[128,...) fusion(bf16[128,8192]{1,0:T(8,128)(2,1)} %param.6, s32[]{:T(128)S(6)} %select_n.35, ...), kind=kLoop, calls=%fused_computation.1 | loop fusion | bytes 3145752 | tf_op jit(solution)/shard_map/dynamic_slice | solution.py:312
  6.7 2.8 %collective-permute-start.3 = (bf16[128,1024]{1,0:T(8,128)(2,1)S(1)}, bf16[128,1024]{1,0:T(8,128)(2,1)S(1)}, u32[]{:S(2)}, u32[]{:S(2)}) collective-permute-start(bf16[128,1024]{1,0:T(8,128)(2,1)S(1)} %get-tuple-element.21), channel_id=1, source_target_pairs={{0,4},{4,8},{8,12},{12,0},{16,28},{20,16},{24,20},{28,24},{32,36},... | collective-permute-start | bytes 786440 | tf_op jit(solution)/shard_map/ppermute | solution.py:234
  10.5 9.2 %collective-permute-done.3.refs_2_.refs_0_ = bf16[128,1024]{1,0:T(8,128)(2,1)S(1)} collective-permute-done((bf16[128,1024]{1,0:T(8,128)(2,1)S(1)}, bf16[128,1024]{1,0:T(8,128)(2,1)S(1)}, u32[]{:S(2)}, u32[]{:S(2)}) %collective-permute-start.3) | collective-permute-done | bytes 262176 | tf_op jit(solution)/shard_map/ppermute | solution.py:234
  19.8 4.6 %collective-permute-done.5.refs_4_.refs_2_ = bf16[128,1024]{1,0:T(8,128)(2,1)S(1)} collective-permute-done((bf16[128,1024]{1,0:T(8,128)(2,1)S(1)}, bf16[128,1024]{1,0:T(8,128)(2,1)S(1)}, u32[]{:S(2)}, u32[]{:S(2)}) %collective-permute-start.5) | collective-permute-done | bytes 262176 | tf_op jit(solution)/shard_map/ppermute | solution.py:234
  24.6 2.7 %collective-permute-start.11 = (bf16[384,1024]{1,0:T(8,128)(2,1)S(1)}, bf16[384,1024]{1,0:T(8,128)(2,1)S(1)}, u32[]{:S(2)}, u32[]{:S(2)}) collective-permute-start(bf16[384,1024]{1,0:T(8,128)(2,1)S(1)} %pack.4.refs_4_), channel_id=1, source_target_pairs={{0,1},{1,2},{2,3},{3,0},{16,19},{17,16},{18,17},{19,18},{32,33},{3... | collective-permute-start | bytes 2359304 | tf_op jit(solution)/shard_map/ppermute | solution.py:234
  27.8 5.1 %collective-permute-done.6.refs_1_.refs_0_ = bf16[128,1024]{1,0:T(8,128)(2,1)S(1)} collective-permute-done((bf16[128,1024]{1,0:T(8,128)(2,1)S(1)}, bf16[128,1024]{1,0:T(8,128)(2,1)S(1)}, u32[]{:S(2)}, u32[]{:S(2)}) %collective-permute-start.6) | collective-permute-done | bytes 262176 | tf_op jit(solution)/shard_map/ppermute | solution.py:234
  33.0 1.7 %collective-permute-start.16 = (bf16[512,512]{1,0:T(8,128)(2,1)S(1)}, bf16[512,512]{1,0:T(8,128)(2,1)}, u32[]{:S(2)}, u32[]{:S(2)}) collective-permute-start(bf16[512,512]{1,0:T(8,128)(2,1)S(1)} %pack.7.refs_0_), channel_id=1, source_target_pairs={{0,4},{4,8},{8,12},{12,0},{16,28},{20,16},{24,20},{28,24},{32,36},... | collective-permute-start | bytes 1572872 | tf_op jit(solution)/shard_map/ppermute | solution.py:234
  34.7 1.3 %collective-permute-start.7 = (bf16[128,1024]{1,0:T(8,128)(2,1)S(1)}, bf16[128,1024]{1,0:T(8,128)(2,1)S(1)}, u32[]{:S(2)}, u32[]{:S(2)}) collective-permute-start(bf16[128,1024]{1,0:T(8,128)(2,1)S(1)} %after.4), channel_id=1, source_target_pairs={{0,8},{4,12},{8,0},{12,4},{16,24},{20,28},{24,16},{28,20},{32,40},... | collective-permute-start | bytes 786440 | tf_op jit(solution)/shard_map/ppermute | solution.py:234
  36.0 7.6 %collective-permute-done.9.refs_4_.refs_7_ = bf16[384,1024]{1,0:T(8,128)(2,1)} collective-permute-done((bf16[384,1024]{1,0:T(8,128)(2,1)S(1)}, bf16[384,1024]{1,0:T(8,128)(2,1)}, u32[]{:S(2)}, u32[]{:S(2)}) %collective-permute-start.9) | collective-permute-done | bytes 786464 | tf_op jit(solution)/shard_map/ppermute | solution.py:234
  43.7 4.1 %collective-permute-done.7.refs_1_ = bf16[128,1024]{1,0:T(8,128)(2,1)S(1)} collective-permute-done((bf16[128,1024]{1,0:T(8,128)(2,1)S(1)}, bf16[128,1024]{1,0:T(8,128)(2,1)S(1)}, u32[]{:S(2)}, u32[]{:S(2)}) %collective-permute-start.7) | collective-permute-done | bytes 262176 | tf_op jit(solution)/shard_map/ppermute | solution.py:234
  47.8 1.1 pack.5.refs_4_
  48.9 1.7 %collective-permute-start.18 = (bf16[512,512]{1,0:T(8,128)(2,1)S(1)}, bf16[512,512]{1,0:T(8,128)(2,1)S(1)}, u32[]{:S(2)}, u32[]{:S(2)}) collective-permute-start(bf16[512,512]{1,0:T(8,128)(2,1)S(1)} %pack.7.refs_0_), channel_id=1, source_target_pairs={{0,12},{4,0},{8,4},{12,8},{16,20},{20,24},{24,28},{28,16},{32,44},... | collective-permute-start | bytes 1572872 | tf_op jit(solution)/shard_map/ppermute | solution.py:234
  50.7 2.8 %collective-permute-start.17 = (bf16[512,512]{1,0:T(8,128)(2,1)}, bf16[512,512]{1,0:T(8,128)(2,1)}, u32[]{:S(2)}, u32[]{:S(2)}) collective-permute-start(bf16[512,512]{1,0:T(8,128)(2,1)} %collective-permute-done.16.refs_1_), channel_id=1, source_target_pairs={{0,4},{4,8},{8,12},{12,0},{16,28},{20,16},{24,20},{28,24},{32,36},... | collective-permute-start | bytes 1572872 | tf_op jit(solution)/shard_map/ppermute | solution.py:234
  53.5 7.9 %collective-permute-done.18.refs_3_ = bf16[512,512]{1,0:T(8,128)(2,1)S(1)} collective-permute-done((bf16[512,512]{1,0:T(8,128)(2,1)S(1)}, bf16[512,512]{1,0:T(8,128)(2,1)S(1)}, u32[]{:S(2)}, u32[]{:S(2)}) %collective-permute-start.18) | collective-permute-done | bytes 524320 | tf_op jit(solution)/shard_map/ppermute | solution.py:234
  62.1 2.6 %collective-permute-start.20 = (bf16[384,768]{1,0:T(8,128)(2,1)}, bf16[384,768]{1,0:T(8,128)(2,1)}, u32[]{:S(2)}, u32[]{:S(2)}) collective-permute-start(bf16[384,768]{1,0:T(8,128)(2,1)} %pack.5.refs_4_), channel_id=1, source_target_pairs={{0,3},{1,0},{2,1},{3,2},{16,17},{17,18},{18,19},{19,16},{32,35},{3... | collective-permute-start | bytes 1769480 | tf_op jit(solution)/shard_map/ppermute | solution.py:234
  68.7 1.5 %order.1.refs_8_ = bf16[2048,512]{1,0:T(8,128)(2,1)S(1)} custom-call(s32[2]{0:T(128)S(1)} %pad_add_fusion.place_ref, bf16[512,512]{1,0:T(8,128)(2,1)S(1)} %pack.7.refs_0_, bf16[512,512]{1,0:T(8,128)(2,1)} %collective-permute-done.16.refs_1_, bf16[512,512]{1,0:T(8,128)(2,1)} %collective-permute-done.17.refs_2_, bf16[512,512]{1,0:T(8,128)(2,1)S(1)} %copy-done.7), custom_call_target="tpu_custom_call" | custom-call | tf_op jit(solution)/shard_map/order/pallas_call | solution.py:334
  70.6 1.5 %collective-permute-start.13 = (bf16[384,256]{1,0:T(8,128)(2,1)S(1)}, bf16[384,256]{1,0:T(8,128)(2,1)S(1)}, u32[]{:S(2)}, u32[]{:S(2)}) collective-permute-start(bf16[384,256]{1,0:T(8,128)(2,1)S(1)} %pack.6.refs_4_), channel_id=1, source_target_pairs={{0,1},{1,2},{2,3},{3,0},{16,19},{17,16},{18,17},{19,18},{32,33},{3... | collective-permute-start | bytes 589832 | tf_op jit(solution)/shard_map/ppermute | solution.py:234
  72.2 8.5 %chunk0.1 = (f32[2048,512]{1,0:T(8,128)}, f32[256,128]{1,0:T(8,128)S(1)}) custom-call(bf16[128,2048]{1,0:T(8,128)(2,1)S(1)} %constant_dynamic-slice_fusion.6.refs_0_, bf16[128,2048]{1,0:T(8,128)(2,1)S(1)} %collective-permute-done.refs_1_.refs_3_, bf16[128,2048]{1,0:T(8,128)(2,1)S(1)} %collective-permute-done.1.refs_3_.refs_2_, ...), custom_call_target="tpu_custom_call" | custom-call | flops 4294967296 | bytes 12582912 | tf_op jit(solution)/shard_map/chunk0/pallas_call | solution.py:133
  80.7 2.6 %collective-permute-done.14.refs_7_ = bf16[384,256]{1,0:T(8,128)(2,1)S(1)} collective-permute-done((bf16[384,256]{1,0:T(8,128)(2,1)S(1)}, bf16[384,256]{1,0:T(8,128)(2,1)S(1)}, u32[]{:S(2)}, u32[]{:S(2)}) %collective-permute-start.14) | collective-permute-done | bytes 196640 | tf_op jit(solution)/shard_map/ppermute | solution.py:234
  83.3 6.9 %chunk4.1 = (f32[2048,512]{1,0:T(8,128)}, f32[192,128]{1,0:T(8,128)S(1)}) custom-call(bf16[128,2048]{1,0:T(8,128)(2,1)S(1)} %constant_dynamic-slice_fusion.6.refs_0_, bf16[128,2048]{1,0:T(8,128)(2,1)S(1)} %collective-permute-done.refs_1_.refs_3_, bf16[128,2048]{1,0:T(8,128)(2,1)S(1)} %collective-permute-done.1.refs_3_.refs_2_, ...), custom_call_target="tpu_custom_call", output_to_operand_aliasing={{0}: (12, {})} | custom-call | flops 3221225472 | bytes 9437184 | tf_op jit(solution)/shard_map/chunk4/pallas_call | solution.py:133
  90.2 2.4 %chunk7.1 = (f32[2048,512]{1,0:T(8,128)}, f32[64,128]{1,0:T(8,128)S(1)}) custom-call(bf16[128,2048]{1,0:T(8,128)(2,1)S(1)} %constant_dynamic-slice_fusion.6.refs_0_, bf16[128,2048]{1,0:T(8,128)(2,1)S(1)} %collective-permute-done.refs_1_.refs_3_, bf16[128,2048]{1,0:T(8,128)(2,1)S(1)} %collective-permute-done.1.refs_3_.refs_2_, ...), custom_call_target="tpu_custom_call", output_to_operand_aliasing={{0}: (12, {})} | custom-call | flops 1073741824 | bytes 3145728 | tf_op jit(solution)/shard_map/chunk7/pallas_call | solution.py:133
  92.7 5.3 %collective-permute-start.21 = (f32[256,128]{1,0:T(8,128)S(1)}, f32[256,128]{1,0:T(8,128)S(1)}, u32[]{:S(2)}, u32[]{:S(2)}) collective-permute-start(f32[256,128]{1,0:T(8,128)S(1)} %get-tuple-element.17), channel_id=1, source_target_pairs={{0,16},{16,0},{32,48},{48,32},{64,80},{80,64},{96,112},{112,96},{1... | collective-permute-start | bytes 393224 | tf_op jit(solution)/shard_map/ppermute | solution.py:249
  99.0 1.6 %collective-permute-start.22 = (f32[256,128]{1,0:T(8,128)S(1)}, f32[256,128]{1,0:T(8,128)S(1)}, u32[]{:S(2)}, u32[]{:S(2)}) collective-permute-start(f32[256,128]{1,0:T(8,128)S(1)} %add.83), channel_id=1, source_target_pairs={{0,32},{16,48},{32,0},{48,16},{64,96},{80,112},{96,64},{112,80},{1... | collective-permute-start | bytes 393224 | tf_op jit(solution)/shard_map/ppermute | solution.py:249
  100.5 3.3 %collective-permute-done.22 = f32[256,128]{1,0:T(8,128)S(1)} collective-permute-done((f32[256,128]{1,0:T(8,128)S(1)}, f32[256,128]{1,0:T(8,128)S(1)}, u32[]{:S(2)}, u32[]{:S(2)}) %collective-permute-start.22) | collective-permute-done | bytes 131104 | tf_op jit(solution)/shard_map/ppermute | solution.py:249
  103.9 5.9 %collective-permute-start.23 = (f32[256,128]{1,0:T(8,128)S(1)}, f32[256,128]{1,0:T(8,128)S(1)}, u32[]{:S(2)}, u32[]{:S(2)}) collective-permute-start(f32[256,128]{1,0:T(8,128)S(1)} %add.84), channel_id=1, source_target_pairs={{0,64},{16,208},{32,96},{48,240},{64,0},{80,144},{96,32},{112,176}... | collective-permute-start | bytes 393224 | tf_op jit(solution)/shard_map/ppermute | solution.py:249
  109.7 3.3 %collective-permute-done.23 = f32[256,128]{1,0:T(8,128)S(1)} collective-permute-done((f32[256,128]{1,0:T(8,128)S(1)}, f32[256,128]{1,0:T(8,128)S(1)}, u32[]{:S(2)}, u32[]{:S(2)}) %collective-permute-start.23) | collective-permute-done | bytes 131104 | tf_op jit(solution)/shard_map/ppermute | solution.py:249
  113.1 1.5 %collective-permute-start.24 = (f32[256,128]{1,0:T(8,128)S(1)}, f32[256,128]{1,0:T(8,128)S(1)}, u32[]{:S(2)}, u32[]{:S(2)}) collective-permute-start(f32[256,128]{1,0:T(8,128)S(1)} %add.85), channel_id=1, source_target_pairs={{0,224},{16,112},{32,192},{48,80},{64,160},{80,48},{96,128},{112,1... | collective-permute-start | bytes 393224 | tf_op jit(solution)/shard_map/ppermute | solution.py:249
  114.6 4.3 %collective-permute-done.24 = f32[256,128]{1,0:T(8,128)S(1)} collective-permute-done((f32[256,128]{1,0:T(8,128)S(1)}, f32[256,128]{1,0:T(8,128)S(1)}, u32[]{:S(2)}, u32[]{:S(2)}) %collective-permute-start.24) | collective-permute-done | bytes 131104 | tf_op jit(solution)/shard_map/ppermute | solution.py:249
  118.9 1.3 %collective-permute-start.25 = (f32[256,128]{1,0:T(8,128)S(1)}, f32[256,128]{1,0:T(8,128)S(1)}, u32[]{:S(2)}, u32[]{:S(2)}) collective-permute-start(f32[256,128]{1,0:T(8,128)S(1)} %add.86), channel_id=1, source_target_pairs={{0,16},{16,0},{32,48},{48,32},{64,80},{80,64},{96,112},{112,96},{1... | collective-permute-start | bytes 393224 | tf_op jit(solution)/shard_map/ppermute | solution.py:249
  121.2 3.0 %spread.1 = bf16[2048,512]{1,0:T(8,128)(2,1)} custom-call(f32[512,128]{1,0:T(8,128)S(1)} %maximum_select_fusion.refs_0_, bf16[640,512]{1,0:T(8,128)(2,1)S(1)} %copy-done.1), custom_call_target="tpu_custom_call" | custom-call | flops 800000000 | bytes 2097152 | tf_op jit(solution)/shard_map/spread/pallas_call | solution.py:172
  (64 shorter events, 9.4 us)
Async XLA Ops:
  1.7 22.6 %collective-permute-start = (bf16[128,2048]{1,0:T(8,128)(2,1)S(1)}, bf16[128,2048]{1,0:T(8,128)(2,1)S(1)}, u32[]{:S(2)}, u32[]{:S(2)}) collective-permute-start(bf16[128,2048]{1,0:T(8,128)(2,1)S(1)} %constant_dynamic-slice_fusion.6.refs_0_), channel_id=1, source_target_pairs={{0,1},{1,2},{2,3},{3,0},{16,19},{17,16},{18,17},{19,18},{32,33},{3... | collective-permute-start | bytes 1572872 | tf_op jit(solution)/shard_map/ppermute | solution.py:234
  5.1 19.2 %collective-permute-start.2 = (bf16[128,2048]{1,0:T(8,128)(2,1)S(1)}, bf16[128,2048]{1,0:T(8,128)(2,1)S(1)}, u32[]{:S(2)}, u32[]{:S(2)}) collective-permute-start(bf16[128,2048]{1,0:T(8,128)(2,1)S(1)} %constant_dynamic-slice_fusion.6.refs_0_), channel_id=1, source_target_pairs={{0,3},{1,0},{2,1},{3,2},{16,17},{17,18},{18,19},{19,16},{32,35},{3... | collective-permute-start | bytes 1572872 | tf_op jit(solution)/shard_map/ppermute | solution.py:234
  6.7 13.1 %collective-permute-start.3 = (bf16[128,1024]{1,0:T(8,128)(2,1)S(1)}, bf16[128,1024]{1,0:T(8,128)(2,1)S(1)}, u32[]{:S(2)}, u32[]{:S(2)}) collective-permute-start(bf16[128,1024]{1,0:T(8,128)(2,1)S(1)} %get-tuple-element.21), channel_id=1, source_target_pairs={{0,4},{4,8},{8,12},{12,0},{16,28},{20,16},{24,20},{28,24},{32,36},... | collective-permute-start | bytes 786440 | tf_op jit(solution)/shard_map/ppermute | solution.py:234
  9.5 10.3 %collective-permute-start.4 = (bf16[128,1024]{1,0:T(8,128)(2,1)S(1)}, bf16[128,1024]{1,0:T(8,128)(2,1)S(1)}, u32[]{:S(2)}, u32[]{:S(2)}) collective-permute-start(bf16[128,1024]{1,0:T(8,128)(2,1)S(1)} %get-tuple-element.20), channel_id=1, source_target_pairs={{0,8},{4,12},{8,0},{12,4},{16,24},{20,28},{24,16},{28,20},{32,40},... | collective-permute-start | bytes 786440 | tf_op jit(solution)/shard_map/ppermute | solution.py:234
  9.8 23.1 %copy-start.8 = (bf16[512,512]{1,0:T(8,128)(2,1)S(1)}, bf16[512,512]{1,0:T(8,128)(2,1)}, u32[]{:S(2)}) copy-start(bf16[512,512]{1,0:T(8,128)(2,1)} %refs_0_.1) | copy-start | bytes 1572868
  9.8 14.5 %collective-permute-start.5 = (bf16[128,1024]{1,0:T(8,128)(2,1)S(1)}, bf16[128,1024]{1,0:T(8,128)(2,1)S(1)}, u32[]{:S(2)}, u32[]{:S(2)}) collective-permute-start(bf16[128,1024]{1,0:T(8,128)(2,1)S(1)} %get-tuple-element.19), channel_id=1, source_target_pairs={{0,12},{4,0},{8,4},{12,8},{16,20},{20,24},{24,28},{28,16},{32,44},... | collective-permute-start | bytes 786440 | tf_op jit(solution)/shard_map/ppermute | solution.py:234
  24.5 10.2 %copy-start.2 = (bf16[384,1024]{1,0:T(8,128)(2,1)}, bf16[384,1024]{1,0:T(8,128)(2,1)S(1)}, u32[]{:S(2)}) copy-start(bf16[384,1024]{1,0:T(8,128)(2,1)S(1)} %pack.4.refs_4_) | copy-start | bytes 2359300
  24.5 19.0 %collective-permute-start.9 = (bf16[384,1024]{1,0:T(8,128)(2,1)S(1)}, bf16[384,1024]{1,0:T(8,128)(2,1)}, u32[]{:S(2)}, u32[]{:S(2)}) collective-permute-start(bf16[384,1024]{1,0:T(8,128)(2,1)S(1)} %pack.4.refs_4_), channel_id=1, source_target_pairs={{0,3},{1,0},{2,1},{3,2},{16,17},{17,18},{18,19},{19,16},{32,35},{3... | collective-permute-start | bytes 2359304 | tf_op jit(solution)/shard_map/ppermute | solution.py:234
  24.6 23.2 %collective-permute-start.11 = (bf16[384,1024]{1,0:T(8,128)(2,1)S(1)}, bf16[384,1024]{1,0:T(8,128)(2,1)S(1)}, u32[]{:S(2)}, u32[]{:S(2)}) collective-permute-start(bf16[384,1024]{1,0:T(8,128)(2,1)S(1)} %pack.4.refs_4_), channel_id=1, source_target_pairs={{0,1},{1,2},{2,3},{3,0},{16,19},{17,16},{18,17},{19,18},{32,33},{3... | collective-permute-start | bytes 2359304 | tf_op jit(solution)/shard_map/ppermute | solution.py:234
  27.3 5.6 %collective-permute-start.6 = (bf16[128,1024]{1,0:T(8,128)(2,1)S(1)}, bf16[128,1024]{1,0:T(8,128)(2,1)S(1)}, u32[]{:S(2)}, u32[]{:S(2)}) collective-permute-start(bf16[128,1024]{1,0:T(8,128)(2,1)S(1)} %after.3), channel_id=1, source_target_pairs={{0,4},{4,8},{8,12},{12,0},{16,28},{20,16},{24,20},{28,24},{32,36},... | collective-permute-start | bytes 786440 | tf_op jit(solution)/shard_map/ppermute | solution.py:234
  33.0 17.7 %collective-permute-start.16 = (bf16[512,512]{1,0:T(8,128)(2,1)S(1)}, bf16[512,512]{1,0:T(8,128)(2,1)}, u32[]{:S(2)}, u32[]{:S(2)}) collective-permute-start(bf16[512,512]{1,0:T(8,128)(2,1)S(1)} %pack.7.refs_0_), channel_id=1, source_target_pairs={{0,4},{4,8},{8,12},{12,0},{16,28},{20,16},{24,20},{28,24},{32,36},... | collective-permute-start | bytes 1572872 | tf_op jit(solution)/shard_map/ppermute | solution.py:234
  34.7 31.1 %copy-start.10 = (s32[1,32,8,16]{1,3,2,0:T(8,128)S(1)}, s32[1,32,8,16]{1,3,2,0:T(8,128)}, u32[]{:S(2)}) copy-start(s32[1,32,8,16]{1,3,2,0:T(8,128)} %param.9) | copy-start | bytes 49156
  34.7 9.0 %collective-permute-start.8 = (bf16[128,1024]{1,0:T(8,128)(2,1)S(1)}, bf16[128,1024]{1,0:T(8,128)(2,1)S(1)}, u32[]{:S(2)}, u32[]{:S(2)}) collective-permute-start(bf16[128,1024]{1,0:T(8,128)(2,1)S(1)} %after.5), channel_id=1, source_target_pairs={{0,12},{4,0},{8,4},{12,8},{16,20},{20,24},{24,28},{28,16},{32,44},... | collective-permute-start | bytes 786440 | tf_op jit(solution)/shard_map/ppermute | solution.py:234
  34.7 13.1 %collective-permute-start.7 = (bf16[128,1024]{1,0:T(8,128)(2,1)S(1)}, bf16[128,1024]{1,0:T(8,128)(2,1)S(1)}, u32[]{:S(2)}, u32[]{:S(2)}) collective-permute-start(bf16[128,1024]{1,0:T(8,128)(2,1)S(1)} %after.4), channel_id=1, source_target_pairs={{0,8},{4,12},{8,0},{12,4},{16,24},{20,28},{24,16},{28,20},{32,40},... | collective-permute-start | bytes 786440 | tf_op jit(solution)/shard_map/ppermute | solution.py:234
  43.6 26.7 %collective-permute-start.10 = (bf16[384,1024]{1,0:T(8,128)(2,1)}, bf16[384,1024]{1,0:T(8,128)(2,1)}, u32[]{:S(2)}, u32[]{:S(2)}) collective-permute-start(bf16[384,1024]{1,0:T(8,128)(2,1)} %collective-permute-done.9.refs_4_.refs_7_), channel_id=1, source_target_pairs={{0,3},{1,0},{2,1},{3,2},{16,17},{17,18},{18,19},{19,16},{32,35},{3... | collective-permute-start | bytes 2359304 | tf_op jit(solution)/shard_map/ppermute | solution.py:234
  47.8 13.6 %copy-start.4 = (bf16[384,1024]{1,0:T(8,128)(2,1)}, bf16[384,1024]{1,0:T(8,128)(2,1)S(1)}, u32[]{:S(2)}) copy-start(bf16[384,1024]{1,0:T(8,128)(2,1)S(1)} %collective-permute-done.11.refs_3_.refs_5_) | copy-start | bytes 2359300
  48.8 15.9 %collective-permute-start.12 = (bf16[384,768]{1,0:T(8,128)(2,1)}, bf16[384,768]{1,0:T(8,128)(2,1)}, u32[]{:S(2)}, u32[]{:S(2)}) collective-permute-start(bf16[384,768]{1,0:T(8,128)(2,1)} %pack.5.refs_4_), channel_id=1, source_target_pairs={{0,1},{1,2},{2,3},{3,0},{16,19},{17,16},{18,17},{19,18},{32,33},{3... | collective-permute-start | bytes 1769480 | tf_op jit(solution)/shard_map/ppermute | solution.py:234
  48.9 12.4 %collective-permute-start.18 = (bf16[512,512]{1,0:T(8,128)(2,1)S(1)}, bf16[512,512]{1,0:T(8,128)(2,1)S(1)}, u32[]{:S(2)}, u32[]{:S(2)}) collective-permute-start(bf16[512,512]{1,0:T(8,128)(2,1)S(1)} %pack.7.refs_0_), channel_id=1, source_target_pairs={{0,12},{4,0},{8,4},{12,8},{16,20},{20,24},{24,28},{28,16},{32,44},... | collective-permute-start | bytes 1572872 | tf_op jit(solution)/shard_map/ppermute | solution.py:234
  50.7 17.0 %collective-permute-start.17 = (bf16[512,512]{1,0:T(8,128)(2,1)}, bf16[512,512]{1,0:T(8,128)(2,1)}, u32[]{:S(2)}, u32[]{:S(2)}) collective-permute-start(bf16[512,512]{1,0:T(8,128)(2,1)} %collective-permute-done.16.refs_1_), channel_id=1, source_target_pairs={{0,4},{4,8},{8,12},{12,0},{16,28},{20,16},{24,20},{28,24},{32,36},... | collective-permute-start | bytes 1572872 | tf_op jit(solution)/shard_map/ppermute | solution.py:234
  53.5 16.8 %collective-permute-start.1 = (bf16[128,2048]{1,0:T(8,128)(2,1)S(1)}, bf16[128,2048]{1,0:T(8,128)(2,1)S(1)}, u32[]{:S(2)}, u32[]{:S(2)}) collective-permute-start(bf16[128,2048]{1,0:T(8,128)(2,1)S(1)} %collective-permute-done.refs_1_.refs_3_), channel_id=1, source_target_pairs={{0,1},{1,2},{2,3},{3,0},{16,19},{17,16},{18,17},{19,18},{32,33},{3... | collective-permute-start | bytes 1572872 | tf_op jit(solution)/shard_map/ppermute | solution.py:234
  62.1 21.2 %collective-permute-start.20 = (bf16[384,768]{1,0:T(8,128)(2,1)}, bf16[384,768]{1,0:T(8,128)(2,1)}, u32[]{:S(2)}, u32[]{:S(2)}) collective-permute-start(bf16[384,768]{1,0:T(8,128)(2,1)} %pack.5.refs_4_), channel_id=1, source_target_pairs={{0,3},{1,0},{2,1},{3,2},{16,17},{17,18},{18,19},{19,16},{32,35},{3... | collective-permute-start | bytes 1769480 | tf_op jit(solution)/shard_map/ppermute | solution.py:234
  64.8 18.5 %collective-permute-start.19 = (bf16[384,768]{1,0:T(8,128)(2,1)}, bf16[384,768]{1,0:T(8,128)(2,1)}, u32[]{:S(2)}, u32[]{:S(2)}) collective-permute-start(bf16[384,768]{1,0:T(8,128)(2,1)} %collective-permute-done.12.refs_5_), channel_id=1, source_target_pairs={{0,1},{1,2},{2,3},{3,0},{16,19},{17,16},{18,17},{19,18},{32,33},{3... | collective-permute-start | bytes 1769480 | tf_op jit(solution)/shard_map/ppermute | solution.py:234
  68.7 3.5 %copy-start = (f32[1,2048,512]{2,1,0:T(8,128)S(1)}, f32[1,2048,512]{2,1,0:T(8,128)}, u32[]{:S(2)}) copy-start(f32[1,2048,512]{2,1,0:T(8,128)} %param.8) | copy-start | bytes 12582916
  70.2 2.0 %copy-start.1 = (bf16[640,512]{1,0:T(8,128)(2,1)S(1)}, bf16[640,512]{1,0:T(8,128)(2,1)}, u32[]{:S(2)}) copy-start(bf16[640,512]{1,0:T(8,128)(2,1)} %constant.46.clone.refs_11_.refs_1_) | copy-start | bytes 1966084
  70.6 19.6 %collective-permute-start.13 = (bf16[384,256]{1,0:T(8,128)(2,1)S(1)}, bf16[384,256]{1,0:T(8,128)(2,1)S(1)}, u32[]{:S(2)}, u32[]{:S(2)}) collective-permute-start(bf16[384,256]{1,0:T(8,128)(2,1)S(1)} %pack.6.refs_4_), channel_id=1, source_target_pairs={{0,1},{1,2},{2,3},{3,0},{16,19},{17,16},{18,17},{19,18},{32,33},{3... | collective-permute-start | bytes 589832 | tf_op jit(solution)/shard_map/ppermute | solution.py:234
  72.1 11.1 %collective-permute-start.14 = (bf16[384,256]{1,0:T(8,128)(2,1)S(1)}, bf16[384,256]{1,0:T(8,128)(2,1)S(1)}, u32[]{:S(2)}, u32[]{:S(2)}) collective-permute-start(bf16[384,256]{1,0:T(8,128)(2,1)S(1)} %pack.6.refs_4_), channel_id=1, source_target_pairs={{0,3},{1,0},{2,1},{3,2},{16,17},{17,18},{18,19},{19,16},{32,35},{3... | collective-permute-start | bytes 589832 | tf_op jit(solution)/shard_map/ppermute | solution.py:234
  83.3 6.9 %collective-permute-start.15 = (bf16[384,256]{1,0:T(8,128)(2,1)S(1)}, bf16[384,256]{1,0:T(8,128)(2,1)S(1)}, u32[]{:S(2)}, u32[]{:S(2)}) collective-permute-start(bf16[384,256]{1,0:T(8,128)(2,1)S(1)} %collective-permute-done.14.refs_7_), channel_id=1, source_target_pairs={{0,3},{1,0},{2,1},{3,2},{16,17},{17,18},{18,19},{19,16},{32,35},{3... | collective-permute-start | bytes 589832 | tf_op jit(solution)/shard_map/ppermute | solution.py:234
  92.7 6.3 %collective-permute-start.21 = (f32[256,128]{1,0:T(8,128)S(1)}, f32[256,128]{1,0:T(8,128)S(1)}, u32[]{:S(2)}, u32[]{:S(2)}) collective-permute-start(f32[256,128]{1,0:T(8,128)S(1)} %get-tuple-element.17), channel_id=1, source_target_pairs={{0,16},{16,0},{32,48},{48,32},{64,80},{80,64},{96,112},{112,96},{1... | collective-permute-start | bytes 393224 | tf_op jit(solution)/shard_map/ppermute | solution.py:249
  99.0 4.9 %collective-permute-start.22 = (f32[256,128]{1,0:T(8,128)S(1)}, f32[256,128]{1,0:T(8,128)S(1)}, u32[]{:S(2)}, u32[]{:S(2)}) collective-permute-start(f32[256,128]{1,0:T(8,128)S(1)} %add.83), channel_id=1, source_target_pairs={{0,32},{16,48},{32,0},{48,16},{64,96},{80,112},{96,64},{112,80},{1... | collective-permute-start | bytes 393224 | tf_op jit(solution)/shard_map/ppermute | solution.py:249
  103.9 9.2 %collective-permute-start.23 = (f32[256,128]{1,0:T(8,128)S(1)}, f32[256,128]{1,0:T(8,128)S(1)}, u32[]{:S(2)}, u32[]{:S(2)}) collective-permute-start(f32[256,128]{1,0:T(8,128)S(1)} %add.84), channel_id=1, source_target_pairs={{0,64},{16,208},{32,96},{48,240},{64,0},{80,144},{96,32},{112,176}... | collective-permute-start | bytes 393224 | tf_op jit(solution)/shard_map/ppermute | solution.py:249
  113.1 5.8 %collective-permute-start.24 = (f32[256,128]{1,0:T(8,128)S(1)}, f32[256,128]{1,0:T(8,128)S(1)}, u32[]{:S(2)}, u32[]{:S(2)}) collective-permute-start(f32[256,128]{1,0:T(8,128)S(1)} %add.85), channel_id=1, source_target_pairs={{0,224},{16,112},{32,192},{48,80},{64,160},{80,48},{96,128},{112,1... | collective-permute-start | bytes 393224 | tf_op jit(solution)/shard_map/ppermute | solution.py:249
  118.9 2.3 %collective-permute-start.25 = (f32[256,128]{1,0:T(8,128)S(1)}, f32[256,128]{1,0:T(8,128)S(1)}, u32[]{:S(2)}, u32[]{:S(2)}) collective-permute-start(f32[256,128]{1,0:T(8,128)S(1)} %add.86), channel_id=1, source_target_pairs={{0,16},{16,0},{32,48},{48,32},{64,80},{80,64},{96,112},{112,96},{1... | collective-permute-start | bytes 393224 | tf_op jit(solution)/shard_map/ppermute | solution.py:249
  (5 other events, 6.8 us)
